TPU v7x, 32 devices: a whole 2x2x4 slice. The times are simulated.
32 devices in a mesh: narrow: 4 (over y, x), wide: 8 (over z, core).
Axes of the slice: x: 2, y: 2, z: 4, core: 2. Of those that a mesh axis runs over, the one named last changes fastest.
Arguments:
- deflation: bfloat16 [8, 3, 16, 64, 256], P(None, None, 'narrow', 'wide'), may hold values from 0.25 to 1
- residual: float32 [3, 16, 64, 256], P(None, 'narrow', 'wide'), may hold values from -1 to 2
- stiffness: float32 [16, 64, 256], P('narrow', 'wide'), may hold values from 0.25 to 2.5
- mass: float32 [16, 64, 256], P('narrow', 'wide'), may hold values from 1 to 4
- stencil: float32 [27, 3, 3], replicated, may hold values from -0.625 to 0.625
- local_inverse: bfloat16 [12, 12, 12, 40, 256], P(None, None, 'narrow', 'wide'), may hold values from -1.75 to 1.75
- inverse_factor: float32 [256, 256], P(('narrow', 'wide')), as said below
- margin_range: int32 [4, 8, 2, 2], P('narrow', 'wide'), may hold values from 0 to 10, as said below
- neighbor_blocks: int32 [4, 8, 9], P('narrow', 'wide'), may hold values from -1 to 31, as said below
Outputs:
- preconditioned: float32 [3, 16, 64, 256], P(None, 'narrow', 'wide')
- coarse_blocks: float32 [4, 8, 9, 8, 8], P('narrow', 'wide')
- coarse_solution: float32 [256], replicated
Inputs may be any that keep to these rules, and one draw needn't show every extreme that they name: `margin_range`: starts are 0 or 1, stops are 5 or 6 along the first dimension and 9 or 10 along the second. `neighbor_blocks`: entry (i, j, (dx + 1) * 3 + dy + 1) is the coarse block number of subdomain (i + dx, j + dy), or -1 if that lies outside the subdomain grid; the numbers of the subdomains are a permutation of 0 to 4 * 8 - 1. `inverse_factor`: zero above the diagonal.
All inputs are finite; a program needn't handle non-finite values.
Results may differ from a plain program's by a relative error of at most 0.0025.
Values may be sent and summed in bfloat16 or wider, within the bound.
A program may use at most 128 MiB of HBM per device.

v0:
```python
import jax
import jax.numpy as jnp
from jax import lax
from jax.sharding import PartitionSpec as P


def extended_2(block, sides, width):
    for axis, dim in sides:
        count = lax.axis_size(axis)
        forward = [(i, i + 1) for i in range(count - 1)]
        backward = [(target, source) for source, target in forward]
        low = lax.ppermute(
            lax.slice_in_dim(block, block.shape[dim] - width, None, axis=dim), axis, forward
        )
        high = lax.ppermute(lax.slice_in_dim(block, 0, width, axis=dim), axis, backward)
        block = jnp.concatenate([low, block, high], axis=dim)
    return block


def side_table(shift, cells):
    where_to = jnp.arange(cells) + shift
    classes = jnp.where(where_to < 0, 0, jnp.where(where_to >= cells, 2, 1))
    return (classes[:, None] == jnp.arange(3)[None, :]).astype(jnp.float32)


def coarse_blocks_of(padded, stencil, stiffness, mass):
    vectors, components, ext_x, ext_y, depth = padded.shape
    cells_x = ext_x - 2
    cells_y = ext_y - 2
    deep = jnp.pad(padded, ((0, 0), (0, 0), (0, 0), (0, 0), (1, 1)))
    own = padded[:, :, 1 : cells_x + 1, 1 : cells_y + 1, :].astype(jnp.float32)
    weighted = own * stiffness
    mass_gram = jnp.einsum("acxyz,bcxyz->abxy", own * mass, own, precision=lax.Precision.HIGHEST)
    blocks = jnp.zeros((3, 3, vectors, vectors), jnp.float32)
    for shift_x in (-1, 0, 1):
        for shift_y in (-1, 0, 1):
            products = jnp.zeros((vectors, vectors, cells_x, cells_y), jnp.float32)
            for shift_z in (-1, 0, 1):
                piece = deep[
                    :,
                    :,
                    1 + shift_x : 1 + shift_x + cells_x,
                    1 + shift_y : 1 + shift_y + cells_y,
                    1 + shift_z : 1 + shift_z + depth,
                ]
                offset = ((shift_x + 1) * 3 + shift_y + 1) * 3 + shift_z + 1
                gram = jnp.einsum(
                    "aixyz,bjxyz->aibjxy",
                    weighted,
                    piece.astype(jnp.float32),
                    precision=lax.Precision.HIGHEST,
                )
                products = products + jnp.einsum(
                    "aibjxy,ij->abxy", gram, stencil[offset], precision=lax.Precision.HIGHEST
                )
            if shift_x == 0 and shift_y == 0:
                products = products + mass_gram
            blocks = blocks + jnp.einsum(
                "abxy,xs,yt->stab",
                products,
                side_table(shift_x, cells_x),
                side_table(shift_y, cells_y),
                precision=lax.Precision.HIGHEST,
            )
    return blocks.reshape(9, vectors, vectors)


def margin_mask(extended, ranges):
    along_x = jnp.arange(extended.shape[1])
    along_y = jnp.arange(extended.shape[2])
    keep_x = (along_x >= ranges[0, 0]) & (along_x < ranges[0, 1])
    keep_y = (along_y >= ranges[1, 0]) & (along_y < ranges[1, 1])
    keep = keep_x[:, None] & keep_y[None, :]
    return jnp.where(keep[None, :, :, None], extended, jnp.zeros_like(extended))


def local_solve(inverse, extended):
    components, ext_x, ext_y, depth = extended.shape
    half_x = ext_x // 2
    half_y = ext_y // 2
    grouped = (
        extended.reshape(components, half_x, 2, half_y, 2, depth)
        .transpose(0, 2, 4, 1, 3, 5)
        .reshape(components * 4, half_x, half_y, depth)
    )
    solved = jnp.einsum("ijxyz,jxyz->ixyz", inverse, grouped, preferred_element_type=jnp.float32)
    solved = (
        solved.reshape(components, 2, 2, half_x, half_y, depth)
        .transpose(0, 3, 1, 4, 2, 5)
        .reshape(components, ext_x, ext_y, depth)
    )
    return solved[:, 1 : ext_x - 1, 1 : ext_y - 1, :]


def body(
    deflation,
    residual,
    stiffness,
    mass,
    stencil,
    local_inverse,
    inverse_factor,
    margin_range,
    neighbor_blocks,
):
    vectors = deflation.shape[0]
    rounded = residual.astype(jnp.bfloat16)
    padded_vectors = extended_2(deflation, (("narrow", 2), ("wide", 3)), 1)
    extended = extended_2(rounded, (("narrow", 1), ("wide", 2)), 1)
    blocks = coarse_blocks_of(padded_vectors, stencil, stiffness, mass)
    rhs_own = jnp.einsum("acxyz,cxyz->a", deflation, rounded, preferred_element_type=jnp.float32)
    extended = margin_mask(extended, margin_range[0, 0])
    local = local_solve(local_inverse, extended)
    listing = neighbor_blocks[0, 0]
    own_block = listing[4]
    total = inverse_factor.shape[1] // vectors
    slots = jnp.arange(total, dtype=jnp.int32)
    own_slot = (slots == own_block).astype(jnp.float32)

    def place(values):
        return lax.psum((own_slot[:, None] * values[None, :]).reshape(-1), ("narrow", "wide"))

    def solve(vector):
        inner = jnp.dot(inverse_factor, vector, precision=lax.Precision.HIGHEST)
        share = jnp.dot(inner, inverse_factor, precision=lax.Precision.HIGHEST)
        return lax.psum(share, ("narrow", "wide"))

    coarse_rhs = place(rhs_own)
    first = solve(coarse_rhs)
    picker = (listing[:, None] == slots[None, :]).astype(jnp.float32)
    near = jnp.dot(picker, first.reshape(total, vectors), precision=lax.Precision.HIGHEST)
    image_own = jnp.einsum("nab,nb->a", blocks, near, precision=lax.Precision.HIGHEST)
    coarse_image = place(image_own)
    coarse_solution = first + solve(coarse_rhs - coarse_image)
    weights = jnp.dot(
        own_slot, coarse_solution.reshape(total, vectors), precision=lax.Precision.HIGHEST
    )
    correction = jnp.sum(weights[:, None, None, None, None] * deflation, axis=0, dtype=jnp.float32)
    preconditioned = local + correction
    return (preconditioned, blocks.reshape(1, 1, 9, vectors, vectors), coarse_solution)


def solution(mesh):
    placed = (
        P(None, None, "narrow", "wide", None),
        P(None, "narrow", "wide", None),
        P("narrow", "wide", None),
        P("narrow", "wide", None),
        P(),
        P(None, None, "narrow", "wide", None),
        P(("narrow", "wide"), None),
        P("narrow", "wide", None, None),
        P("narrow", "wide", None),
    )
    return jax.shard_map(
        body,
        mesh=mesh,
        in_specs=placed,
        out_specs=(P(None, "narrow", "wide", None), P("narrow", "wide", None, None, None), P()),
        check_vma=False,
    )
```

profile of v0, /device:TPU:0, one launch (start us, length us, event | category | flops | bytes accessed | tf_op | source)
XLA Modules:
  0.0 436.5 jit_solution(18175033978042229280)
XLA Ops:
  1.7 4.8 %collective-permute-start = (bf16[3,1,8,256]{3,2,1,0:T(8,128)(2,1)S(1)}, bf16[3,1,8,256]{3,2,1,0:T(8,128)(2,1)S(1)}, u32[]{:S(2)}, u32[]{:S(2)}) collective-permute-start(bf16[3,1,8,256]{3,2,1,0:T(8,128)(2,1)S(1)} %get-tuple-element.41), channel_id=1, source_target_pairs={{0,8},{8,16},{16,24},{1,9},{9,17},{17,25},{2,10},{10,18},{18,26},{... | collective-permute-start | bytes 36872 | tf_op jit(solution)/shard_map/ppermute | solution.py:12
  10.4 5.2 %collective-permute-start.4 = (bf16[8,3,1,8,256]{4,0,1,3,2:T(8,128)(2,1)S(1)}, bf16[8,3,1,8,256]{4,0,1,3,2:T(8,128)(2,1)S(1)}, u32[]{:S(2)}, u32[]{:S(2)}) collective-permute-start(bf16[8,3,1,8,256]{4,0,1,3,2:T(8,128)(2,1)S(1)} %get-tuple-element.38), channel_id=1, source_target_pairs={{0,8},{8,16},{16,24},{1,9},{9,17},{17,25},{2,10},{10,18},{18,26},{... | collective-permute-start | bytes 294920 | tf_op jit(solution)/shard_map/ppermute | solution.py:12
  23.2 40.5 %psum.28 = f32[256]{0:T(256)S(1)} all-reduce(f32[256]{0:T(256)S(1)} %mul.59), channel_id=1, replica_groups=mesh['narrow'=4,'wide'=8] {'narrow','wide'}, use_global_device_ids=true, to_apply=%region_0.1 | all-reduce | flops 256 | bytes 2048 | tf_op jit(solution)/shard_map/psum | solution.py:121
  64.2 41.4 %psum.29 = f32[256]{0:T(256)S(1)} all-reduce(f32[256]{0:T(256)S(1)} %bitcast.505), channel_id=1, replica_groups=mesh['narrow'=4,'wide'=8] {'narrow','wide'}, use_global_device_ids=true, to_apply=%region_1.2 | all-reduce | flops 256 | bytes 2048 | tf_op jit(solution)/shard_map/psum | solution.py:126
  136.2 4.9 %collective-permute-start.6 = (bf16[8,3,6,1,256]{4,0,3,2,1:T(8,128)(2,1)}, bf16[8,3,6,1,256]{4,0,3,2,1:T(8,128)(2,1)S(1)}, u32[]{:S(2)}, u32[]{:S(2)}) collective-permute-start(bf16[8,3,6,1,256]{4,0,3,2,1:T(8,128)(2,1)} %copy.26), channel_id=1, source_target_pairs={{0,1},{1,2},{2,3},{3,4},{4,5},{5,6},{6,7},{8,9},{9,10},{10,11},{11... | collective-permute-start | bytes 221192 | tf_op jit(solution)/shard_map/ppermute | solution.py:12
  141.1 3.6 convolution_bitcast_fusion.22
  147.4 4.6 %convolution_bitcast_fusion.4 = f32[8,3,8,3,4,8]{0,2,1,3,5,4:T(8,128)} fusion(bf16[8,3,1,8,256]{4,0,1,3,2:T(8,128)(2,1)} %copy-done.41, bf16[8,3,4,8,256]{4,0,1,3,2:T(8,128)(2,1)} %copy-done.24, f32[8,3,4,8,256,1]{4,3,2,1,0,5:T(8,128)S(1)} %get-tuple-element.36), kind=kOutput, calls=%fused_computation.8 | convolution fusion | flops 57409536 | bytes 1351680 | tf_op jit(solution)/shard_map/aixyz,bjxyz->aibjxy/dot_general | solution.py:47
  161.2 3.3 convolution_bitcast_fusion.24
  164.5 3.6 convolution_bitcast_fusion.23
  168.1 3.3 convolution_bitcast_fusion.21
  171.4 3.7 convolution_bitcast_fusion.20
  175.1 3.3 convolution_bitcast_fusion.18
  178.4 3.6 convolution_bitcast_fusion.17
  185.2 3.7 convolution_bitcast_fusion.11
  192.1 3.8 convolution_bitcast_fusion.8
  199.2 3.6 convolution_bitcast_fusion.5
  202.7 3.3 convolution_bitcast_fusion.3
  206.0 3.6 convolution_bitcast_fusion.2
  209.6 3.3 convolution_bitcast_fusion
  212.9 4.0 convolution_bitcast_fusion.26
  242.9 3.3 copy.133
  267.4 3.6 convolution_bitcast_fusion.1
  351.2 41.2 %psum.30 = f32[256]{0:T(256)S(1)} all-reduce(f32[256]{0:T(256)S(1)} %mul.66), channel_id=1, replica_groups=mesh['narrow'=4,'wide'=8] {'narrow','wide'}, use_global_device_ids=true, to_apply=%region_2.3 | all-reduce | flops 256 | bytes 2048 | tf_op jit(solution)/shard_map/psum | solution.py:121
  392.7 40.4 %psum.31 = f32[256]{0:T(256)S(1)} all-reduce(f32[256]{0:T(256)S(1)} %bitcast.506), channel_id=1, replica_groups=mesh['narrow'=4,'wide'=8] {'narrow','wide'}, use_global_device_ids=true, to_apply=%region_3.4 | all-reduce | flops 256 | bytes 2048 | tf_op jit(solution)/shard_map/psum | solution.py:126
  (346 shorter events, 194.7 us)
Async XLA Ops:
  0.6 63.1 %copy-start = (f32[8,256]{1,0:T(8,128)S(1)}, f32[8,256]{1,0:T(8,128)}, u32[]{:S(2)}) copy-start(f32[8,256]{1,0:T(8,128)} %param.15) | copy-start | bytes 24580
  0.6 20.0 %copy-start.42 = (f32[3,4,8,256]{3,2,1,0:T(8,128)S(1)}, f32[3,4,8,256]{3,2,1,0:T(8,128)}, u32[]{:S(2)}) copy-start(f32[3,4,8,256]{3,2,1,0:T(8,128)} %param.10) | copy-start | bytes 294916
  0.7 21.9 %copy-start.1 = (bf16[8,3,4,8,256]{4,3,2,1,0:T(8,128)(2,1)S(1)}, bf16[8,3,4,8,256]{4,3,2,1,0:T(8,128)(2,1)}, u32[]{:S(2)}) copy-start(bf16[8,3,4,8,256]{4,3,2,1,0:T(8,128)(2,1)} %param.9) | copy-start | bytes 1179652
  0.7 20.0 %copy-start.82 = (s32[1,1,9]{2,1,0:T(1,128)S(1)}, s32[1,1,9]{2,1,0:T(1,128)}, u32[]{:S(2)}) copy-start(s32[1,1,9]{2,1,0:T(1,128)} %param.17) | copy-start | bytes 112
  0.7 21.1 %copy-start.79 = (s32[1,1,2,2]{3,2,1,0:T(2,128)S(1)}, s32[1,1,2,2]{3,2,1,0:T(2,128)}, u32[]{:S(2)}) copy-start(s32[1,1,2,2]{3,2,1,0:T(2,128)} %param.16) | copy-start | bytes 52
  0.7 108.0 %copy-start.44 = (f32[4,8,256]{2,1,0:T(8,128)S(1)}, f32[4,8,256]{2,1,0:T(8,128)}, u32[]{:S(2)}) copy-start(f32[4,8,256]{2,1,0:T(8,128)} %param.12) | copy-start | bytes 98308
  0.7 108.0 %copy-start.45 = (f32[4,8,256]{2,1,0:T(8,128)S(1)}, f32[4,8,256]{2,1,0:T(8,128)}, u32[]{:S(2)}) copy-start(f32[4,8,256]{2,1,0:T(8,128)} %param.11) | copy-start | bytes 98308
  1.7 111.7 %collective-permute-start = (bf16[3,1,8,256]{3,2,1,0:T(8,128)(2,1)S(1)}, bf16[3,1,8,256]{3,2,1,0:T(8,128)(2,1)S(1)}, u32[]{:S(2)}, u32[]{:S(2)}) collective-permute-start(bf16[3,1,8,256]{3,2,1,0:T(8,128)(2,1)S(1)} %get-tuple-element.41), channel_id=1, source_target_pairs={{0,8},{8,16},{16,24},{1,9},{9,17},{17,25},{2,10},{10,18},{18,26},{... | collective-permute-start | bytes 36872 | tf_op jit(solution)/shard_map/ppermute | solution.py:12
  6.5 106.8 %collective-permute-start.1 = (bf16[3,1,8,256]{3,2,1,0:T(8,128)(2,1)S(1)}, bf16[3,1,8,256]{3,2,1,0:T(8,128)(2,1)S(1)}, u32[]{:S(2)}, u32[]{:S(2)}) collective-permute-start(bf16[3,1,8,256]{3,2,1,0:T(8,128)(2,1)S(1)} %get-tuple-element.42), channel_id=1, source_target_pairs={{8,0},{16,8},{24,16},{9,1},{17,9},{25,17},{10,2},{18,10},{26,18},{... | collective-permute-start | bytes 36872 | tf_op jit(solution)/shard_map/ppermute | solution.py:15
  9.0 132.0 %copy-start.24 = (bf16[8,3,4,8,256]{4,0,1,3,2:T(8,128)(2,1)}, bf16[8,3,4,8,256]{4,0,1,3,2:T(8,128)(2,1)S(1)}, u32[]{:S(2)}) copy-start(bf16[8,3,4,8,256]{4,0,1,3,2:T(8,128)(2,1)S(1)} %copy.23) | copy-start | bytes 1179652
  9.1 124.5 %collective-permute-start.5 = (bf16[8,3,1,8,256]{4,0,1,3,2:T(8,128)(2,1)S(1)}, bf16[8,3,1,8,256]{4,0,1,3,2:T(8,128)(2,1)S(1)}, u32[]{:S(2)}, u32[]{:S(2)}) collective-permute-start(bf16[8,3,1,8,256]{4,0,1,3,2:T(8,128)(2,1)S(1)} %get-tuple-element.37), channel_id=1, source_target_pairs={{8,0},{16,8},{24,16},{9,1},{17,9},{25,17},{10,2},{18,10},{26,18},{... | collective-permute-start | bytes 294920 | tf_op jit(solution)/shard_map/ppermute | solution.py:15
  10.4 122.9 %collective-permute-start.4 = (bf16[8,3,1,8,256]{4,0,1,3,2:T(8,128)(2,1)S(1)}, bf16[8,3,1,8,256]{4,0,1,3,2:T(8,128)(2,1)S(1)}, u32[]{:S(2)}, u32[]{:S(2)}) collective-permute-start(bf16[8,3,1,8,256]{4,0,1,3,2:T(8,128)(2,1)S(1)} %get-tuple-element.38), channel_id=1, source_target_pairs={{0,8},{8,16},{16,24},{1,9},{9,17},{17,25},{2,10},{10,18},{18,26},{... | collective-permute-start | bytes 294920 | tf_op jit(solution)/shard_map/ppermute | solution.py:12
  105.7 7.1 %copy-start.46 = (f32[256]{0:T(256)}, f32[256]{0:T(256)S(1)}, u32[]{:S(2)}) copy-start(f32[256]{0:T(256)S(1)} %psum.29) | copy-start | bytes 3076
  113.4 16.0 %collective-permute-start.2 = (bf16[3,6,1,256]{3,2,1,0:T(2,128)(2,1)S(1)}, bf16[3,6,1,256]{3,2,1,0:T(2,128)(2,1)S(1)}, u32[]{:S(2)}, u32[]{:S(2)}) collective-permute-start(bf16[3,6,1,256]{3,2,1,0:T(2,128)(2,1)S(1)} %get-tuple-element.39), channel_id=1, source_target_pairs={{0,1},{1,2},{2,3},{3,4},{4,5},{5,6},{6,7},{8,9},{9,10},{10,11},{11... | collective-permute-start | bytes 27656 | tf_op jit(solution)/shard_map/ppermute | solution.py:12
  114.7 14.7 %collective-permute-start.3 = (bf16[3,6,1,256]{3,2,1,0:T(2,128)(2,1)S(1)}, bf16[3,6,1,256]{3,2,1,0:T(2,128)(2,1)S(1)}, u32[]{:S(2)}, u32[]{:S(2)}) collective-permute-start(bf16[3,6,1,256]{3,2,1,0:T(2,128)(2,1)S(1)} %get-tuple-element.40), channel_id=1, source_target_pairs={{1,0},{2,1},{3,2},{4,3},{5,4},{6,5},{7,6},{9,8},{10,9},{11,10},{12... | collective-permute-start | bytes 27656 | tf_op jit(solution)/shard_map/ppermute | solution.py:15
  133.6 7.5 %copy-start.41 = (bf16[8,3,1,8,256]{4,0,1,3,2:T(8,128)(2,1)}, bf16[8,3,1,8,256]{4,0,1,3,2:T(8,128)(2,1)S(1)}, u32[]{:S(2)}) copy-start(bf16[8,3,1,8,256]{4,0,1,3,2:T(8,128)(2,1)S(1)} %collective-permute-done.5) | copy-start | bytes 294916
  134.9 25.7 %collective-permute-start.7 = (bf16[8,3,6,1,256]{4,0,3,2,1:T(8,128)(2,1)}, bf16[8,3,6,1,256]{4,0,3,2,1:T(8,128)(2,1)S(1)}, u32[]{:S(2)}, u32[]{:S(2)}) collective-permute-start(bf16[8,3,6,1,256]{4,0,3,2,1:T(8,128)(2,1)} %copy.27), channel_id=1, source_target_pairs={{1,0},{2,1},{3,2},{4,3},{5,4},{6,5},{7,6},{9,8},{10,9},{11,10},{12... | collective-permute-start | bytes 221192 | tf_op jit(solution)/shard_map/ppermute | solution.py:15
  136.2 24.4 %collective-permute-start.6 = (bf16[8,3,6,1,256]{4,0,3,2,1:T(8,128)(2,1)}, bf16[8,3,6,1,256]{4,0,3,2,1:T(8,128)(2,1)S(1)}, u32[]{:S(2)}, u32[]{:S(2)}) collective-permute-start(bf16[8,3,6,1,256]{4,0,3,2,1:T(8,128)(2,1)} %copy.26), channel_id=1, source_target_pairs={{0,1},{1,2},{2,3},{3,4},{4,5},{5,6},{6,7},{8,9},{9,10},{10,11},{11... | collective-permute-start | bytes 221192 | tf_op jit(solution)/shard_map/ppermute | solution.py:12
  336.9 6.6 %copy-start.74 = (s32[4]{0:T(128)S(1)}, s32[4]{0:T(128)}, u32[]{:S(2)}) copy-start(s32[4]{0:T(128)} %compare_select_fusion.2) | copy-start | bytes 52
  340.0 6.1 %copy-start.39 = (f32[1,8,8,4,8,1]{4,0,5,3,2,1:T(1,128)S(1)}, f32[1,8,8,4,8,1]{4,0,5,3,2,1:T(1,128)}, u32[]{:S(2)}) copy-start(f32[1,8,8,4,8,1]{4,0,5,3,2,1:T(1,128)} %fusion.192) | copy-start | bytes 24580
  341.2 6.1 %copy-start.73 = (s32[4]{0:T(128)S(1)}, s32[4]{0:T(128)}, u32[]{:S(2)}) copy-start(s32[4]{0:T(128)} %compare_select_fusion.1) | copy-start | bytes 52
  341.4 6.2 %copy-start.50 = (f32[3,3,1,1,1,1]{1,2,0,5,4,3:T(1,128)S(1)}, f32[3,3,1,1,1,1]{1,2,0,5,4,3:T(1,128)}, u32[]{:S(2)}) copy-start(f32[3,3,1,1,1,1]{1,2,0,5,4,3:T(1,128)} %reshape.326) | copy-start | bytes 112
  346.1 46.4 %copy-start.49 = (f32[256]{0:T(256)S(1)}, f32[256]{0:T(256)}, u32[]{:S(2)}) copy-start(f32[256]{0:T(256)} %copy-done.48) | copy-start | bytes 3076
  346.1 87.0 %copy-start.47 = (f32[256]{0:T(256)S(1)}, f32[256]{0:T(256)}, u32[]{:S(2)}) copy-start(f32[256]{0:T(256)} %copy-done.46) | copy-start | bytes 3076
  (67 other events, 253.0 us)
where the time goes:
time: 443 us; the launch traced here: 437 us
  blocking collectives  164 us (37%)
  matrix products  153 us (35%)
  local copies, waits for them, and re-layouts  82.4 us (19%)
  starting transfers between devices  21.4 us (5%)
  other arithmetic  13.8 us (3%)
    dot_general x27, matrix products, coarse_blocks_of(): jnp.einsum('aixyz,bjxyz->aibjxy', weighted, piece.astype(jnp.float32), pr...  87.9 us
    psum x2, blocking collectives, solve(): return lax.psum(share, ('narrow', 'wide'))  81.8 us
    psum x2, blocking collectives, place(): lax.psum((own_slot[:, None] * values[None, :]).reshape(-1), ('narrow', 'w...  81.7 us
    transpose x24, local copies, waits for them, and re-layouts, coarse_blocks_of(): jnp.einsum('aixyz,bjxyz->aibjxy', weighted, piece.astype(jnp.float32), pr...  58.1 us
    dot_general x24, matrix products, coarse_blocks_of(): jnp.einsum('aibjxy,ij->abxy', gram, stencil[offset], precision=lax.Precis...  52.1 us
    ppermute x4, starting transfers between devices, extended_2(): lax.ppermute(lax.slice_in_dim(block, block.shape[dim] - width, None, axis...  16.2 us
    squeeze x24, local copies, waits for them, and re-layouts, coarse_blocks_of(): stencil[offset]  12.5 us
    dot_general x18, matrix products, coarse_blocks_of(): jnp.einsum('abxy,xs,yt->stab', products, side_table(shift_x, cells_x), si...  9.87 us
  transfers between devices with their start and end apart: 8, of which 0 were waited for; matrix products, arithmetic and copies ran while one was open for 12% of the time, Pallas kernels for 0%

commit v1 on v0

v1 whole, which is shorter than its diff:
```python
import functools

import jax
import jax.numpy as jnp
import numpy as np
from jax import lax
from jax.experimental import pallas as pl
from jax.experimental.pallas import tpu as pltpu
from jax.sharding import PartitionSpec as P

F32 = jnp.float32
BF16 = jnp.bfloat16
HIGHEST = lax.Precision.HIGHEST
MESH = pl.DeviceIdType.MESH


def pad_to(count, unit):
    return -(-count // unit) * unit


def stencil_places(comps, nx, ny):
    rows = []
    for j in range(comps):
        rows += [(j, x, y) for x in range(nx) for y in range(ny)]
    for x in (-1, nx):
        rows += [(j, x, y) for j in range(comps) for y in range(ny)]
    for y in (-1, ny):
        face = [(j, x, y) for j in range(comps) for x in range(nx)]
        rows += face + [None] * (pad_to(len(face), 8) - len(face))
    corners = [(j, x, y) for x in (-1, nx) for y in (-1, ny) for j in range(comps)]
    rows += corners + [None] * (pad_to(len(corners), 8) - len(corners))
    cells = comps * nx * ny
    table = np.full((len(rows), 3 * cells), -1, np.int32)
    for r, row in enumerate(rows):
        if row is None:
            continue
        j, x, y = row
        for oz in range(3):
            for i in range(comps):
                for px in range(nx):
                    for py in range(ny):
                        dx, dy = x - px, y - py
                        if abs(dx) <= 1 and abs(dy) <= 1:
                            column = oz * cells + i * nx * ny + px * ny + py
                            table[r, column] = j * 9 + (dx + 1) * 3 + dy + 1
    return table


def split(values):
    high = values.astype(BF16)
    return high, (values - high.astype(F32)).astype(BF16)


def iota(shape, axis):
    return lax.broadcasted_iota(jnp.int32, shape, axis)


def load(ref, *at):
    return jnp.concatenate([ref[(h,) + at] for h in range(ref.shape[0])], axis=-1)


def store(ref, values, *at):
    for h in range(ref.shape[0]):
        ref[(h,) + at] = values[:, h * 128 : (h + 1) * 128]


def gram(left, right):
    dims = (((1,), (1,)), ((), ()))
    high, low = split(left)
    return lax.dot_general(high, right, dims, preferred_element_type=F32) + lax.dot_general(
        low, right, dims, preferred_element_type=F32
    )


def kernel(
    narrow,
    wide,
    vectors,
    comps,
    nx,
    ny,
    depth,
    deflation,
    residual,
    stiffness,
    mass,
    places,
    coupling,
    inverse_hbm,
    factor,
    margins,
    listing,
    out,
    blocks_out,
    solution_out,
    inverse,
    d32,
    r32,
    t32,
    s_parts,
    w_parts,
    stage,
    ext,
    loc,
    send_x,
    send_y,
    send_c,
    recv_x,
    recv_y,
    recv_c,
    factors,
    message,
    slots,
    inverse_sem,
    send_sems,
    recv_sems,
    wave_send,
    wave_recv,
):
    n = narrow * wide
    order = factor.shape[1]
    row = lax.axis_index("narrow")
    column = lax.axis_index("wide")
    me = row * wide + column
    cells = nx * ny
    own_rows = comps * cells

    def target_of(k):
        t = lax.rem(me + k, n)
        return (t // wide, lax.rem(t, wide))

    barrier = pltpu.get_barrier_semaphore()

    def greet(k, carry):
        pl.semaphore_signal(barrier, inc=1, device_id=target_of(k), device_id_type=MESH)
        return carry

    lax.fori_loop(1, n, greet, 0)

    inverse_copy = pltpu.make_async_copy(inverse_hbm, inverse, inverse_sem)
    inverse_copy.start()

    rounded = residual[...].astype(BF16).astype(F32).reshape(own_rows, depth)
    store(r32, rounded, pl.ds(0, own_rows))
    sums = []
    for a in range(vectors):
        d = deflation[a].astype(F32).reshape(own_rows, depth)
        store(d32, d, pl.ds(a * own_rows, own_rows))
        sums.append(jnp.sum(d * rounded, axis=0, keepdims=True))
    rhs_column = jnp.sum(jnp.concatenate(sums, axis=0), axis=1, keepdims=True)
    own_block = listing[0, 0, 4]
    own_place = iota((vectors, order), 1) == own_block * vectors + iota((vectors, order), 0)

    def placed(values):
        return jnp.sum(jnp.where(own_place, values, 0.0), axis=0, keepdims=True)

    message[0] = placed(rhs_column)

    x_rows = comps * ny
    y_rows = comps * nx
    for side, x in enumerate((0, nx - 1)):
        face = [
            load(d32, pl.ds((a * comps + j) * cells + x * ny, ny))
            for a in range(vectors)
            for j in range(comps)
        ]
        send_x[side, pl.ds(0, vectors * x_rows), :] = jnp.concatenate(face, axis=0).astype(BF16)
        stage[...] = jnp.zeros_like(stage)
        for j in range(comps):
            stage[pl.ds(j * ny, ny), :] = load(r32, pl.ds(j * cells + x * ny, ny))
        send_x[side, pl.ds(vectors * x_rows, 32), :] = stage[...].astype(BF16)
    for side, y in enumerate((0, ny - 1)):
        face = load(d32, pl.ds(y, vectors * y_rows, stride=ny))
        send_y[side, pl.ds(0, vectors * y_rows), :] = face.astype(BF16)
        stage[...] = jnp.zeros_like(stage)
        stage[pl.ds(0, y_rows), :] = load(r32, pl.ds(y, y_rows, stride=ny))
        send_y[side, pl.ds(vectors * y_rows, 16), :] = stage[pl.ds(0, 16), :].astype(BF16)
    for side_x, x in enumerate((0, nx - 1)):
        for side_y, y in enumerate((0, ny - 1)):
            stage[...] = jnp.zeros_like(stage)
            at = x * ny + y
            stage[pl.ds(0, vectors * comps), :] = load(d32, pl.ds(at, vectors * comps, stride=cells))
            stage[pl.ds(vectors * comps, comps), :] = load(r32, pl.ds(at, comps, stride=cells))
            send_c[side_x * 2 + side_y] = stage[...].astype(BF16)

    pl.semaphore_wait(barrier, n - 1)

    def wave(number):
        def one(k, carry):
            pltpu.make_async_remote_copy(
                src_ref=message.at[number],
                dst_ref=slots.at[number, k - 1],
                send_sem=wave_send.at[number],
                recv_sem=wave_recv.at[number],
                device_id=target_of(k),
                device_id_type=MESH,
            ).start()
            return carry

        lax.fori_loop(1, n, one, 0)

    def wave_sum(number):
        pltpu.make_async_copy(slots.at[number], slots.at[number], wave_recv.at[number]).wait()
        return lax.fori_loop(
            0,
            n - 1,
            lambda k, total: total + slots[number, k],
            message[number],
            unroll=n <= 32,
        )

    wave(0)

    def copies():
        found = []
        for side, shift in enumerate((-1, 1)):
            found.append((send_x.at[side], recv_x.at[1 - side], recv_x.at[side], shift, 0))
        for side, shift in enumerate((-1, 1)):
            found.append((send_y.at[side], recv_y.at[1 - side], recv_y.at[side], 0, shift))
        for side_x, shift_x in enumerate((-1, 1)):
            for side_y, shift_y in enumerate((-1, 1)):
                at = side_x * 2 + side_y
                found.append((send_c.at[at], recv_c.at[3 - at], recv_c.at[at], shift_x, shift_y))
        return found

    opposite = (1, 0, 3, 2, 7, 6, 5, 4)

    def inside(shift_x, shift_y):
        along_x = (row + shift_x >= 0) & (row + shift_x < narrow)
        along_y = (column + shift_y >= 0) & (column + shift_y < wide)
        return along_x & along_y

    def face_copy(k, source, target, shift_x, shift_y):
        return pltpu.make_async_remote_copy(
            src_ref=source,
            dst_ref=target,
            send_sem=send_sems.at[k],
            recv_sem=recv_sems.at[opposite[k]],
            device_id=(row + shift_x, column + shift_y),
            device_id_type=MESH,
        )

    for k, (source, target, _, shift_x, shift_y) in enumerate(copies()):

        @pl.when(inside(shift_x, shift_y))
        def _(k=k, source=source, target=target, shift_x=shift_x, shift_y=shift_y):
            face_copy(k, source, target, shift_x, shift_y).start()

    factors[me] = factor[...]

    def send_factor(k, carry):
        pltpu.make_async_remote_copy(
            src_ref=factor,
            dst_ref=factors.at[me],
            send_sem=wave_send.at[2],
            recv_sem=wave_recv.at[2],
            device_id=target_of(k),
            device_id_type=MESH,
        ).start()
        return carry

    lax.fori_loop(1, n, send_factor, 0)

    total_rows = places.shape[0]
    fixed = own_rows + 2 * x_rows
    chunks = [(j * cells, cells, j) for j in range(comps)]
    for side in range(2):
        chunks += [(own_rows + side * x_rows + j * ny, ny, j) for j in range(comps)]
    chunks.append((fixed, total_rows - fixed, None))
    for start, size, j in chunks:
        here = places[pl.ds(start, size), :]
        value = jnp.zeros(here.shape, F32)
        for e in range(comps * 9) if j is None else range(j * 9, j * 9 + 9):
            value = jnp.where(here == e, coupling[pl.ds(e, 1), :], value)
        s_parts[pl.ds(start, size), :] = value
    s_high, s_low = split(s_parts[...])

    lane = iota((own_rows, depth), 1)
    scale = jnp.concatenate([stiffness[...].reshape(cells, depth)] * comps, axis=0)
    weight = jnp.concatenate([mass[...].reshape(cells, depth)] * comps, axis=0)
    for a in range(vectors):
        d = load(d32, pl.ds(a * own_rows, own_rows))
        w = d * scale
        before = jnp.where(lane == depth - 1, 0.0, pltpu.roll(w, depth - 1, axis=1))
        after = jnp.where(lane == 0, 0.0, pltpu.roll(w, 1, axis=1))
        for oz, shifted in enumerate((before, w, after)):
            high, low = split(shifted)
            w_parts[a % 2, 0, pl.ds(oz * own_rows, own_rows), :] = high
            w_parts[a % 2, 1, pl.ds(oz * own_rows, own_rows), :] = low
        high = w_parts[a % 2, 0]
        low = w_parts[a % 2, 1]
        image = (
            jnp.dot(s_high, high, preferred_element_type=F32)
            + jnp.dot(s_high, low, preferred_element_type=F32)
            + jnp.dot(s_low, high, preferred_element_type=F32)
        )
        t32[a] = image
        t32[a, pl.ds(0, own_rows), :] = image[:own_rows] + weight * d

    width = 9 * vectors

    def picked(product, left_of, right_of, left_size):
        r = iota(product.shape, 0)
        c = iota(product.shape, 1)
        kept = jnp.where(left_of(r) == right_of(c), product, 0.0)
        return jnp.sum(kept.reshape(vectors, left_size, product.shape[1]), axis=1)

    def folded(values, lane_of):
        shape = (values.shape[1], width)
        chosen = (lane_of(iota(shape, 0)) == iota(shape, 1)).astype(F32)
        return jnp.dot(values, chosen, preferred_element_type=F32, precision=HIGHEST)

    total = None
    for j in range(comps):
        left = t32[:, pl.ds(j * cells, cells), :].reshape(vectors * cells, depth)
        right = jnp.concatenate(
            [load(d32, pl.ds((b * comps + j) * cells, cells)) for b in range(vectors)], axis=0
        ).astype(BF16)
        part = gram(left, right)
        total = part if total is None else total + part
    chosen = picked(total, lambda r: lax.rem(r, cells), lambda c: lax.rem(c, cells), cells)
    blocks = folded(chosen, lambda c: 4 * vectors + c // cells)

    for k, (source, target, landing, shift_x, shift_y) in enumerate(copies()):

        @pl.when(inside(shift_x, shift_y))
        def _(k=k, source=source, landing=landing, shift_x=shift_x, shift_y=shift_y):
            pltpu.make_async_remote_copy(
                src_ref=source,
                dst_ref=landing,
                send_sem=send_sems.at[k],
                recv_sem=recv_sems.at[k],
                device_id=(row + shift_x, column + shift_y),
                device_id_type=MESH,
            ).wait()

        @pl.when(jnp.logical_not(inside(shift_x, shift_y)))
        def _(landing=landing):
            landing[...] = jnp.zeros(landing.shape, BF16)

    for side in range(2):
        n_class = (1 if side == 0 else 7) * vectors
        left = t32[:, pl.ds(own_rows + side * x_rows, x_rows), :].reshape(vectors * x_rows, depth)
        part = gram(left, recv_x[side, pl.ds(0, vectors * x_rows), :])
        chosen = picked(part, lambda r: lax.rem(r, x_rows), lambda c: lax.rem(c, x_rows), x_rows)
        blocks += folded(chosen, lambda c, at=n_class: at + c // x_rows)
    y_padded = pad_to(y_rows, 8)
    for side in range(2):
        n_class = (3 if side == 0 else 5) * vectors
        left = t32[:, pl.ds(fixed + side * y_padded, y_padded), :]
        left = left.reshape(vectors * y_padded, depth)
        part = gram(left, recv_y[side, pl.ds(0, vectors * y_rows), :])
        chosen = picked(
            part, lambda r: lax.rem(r, y_padded), lambda c: lax.rem(c, y_rows), y_padded
        )
        blocks += folded(chosen, lambda c, at=n_class: at + c // y_rows)
    c_padded = pad_to(4 * comps, 8)
    left = t32[:, pl.ds(fixed + 2 * y_padded, c_padded), :].reshape(vectors * c_padded, depth)
    part = gram(left, recv_c[...].reshape(4 * 32, depth))

    def corner_row(c):
        at = lax.rem(c, 32)
        return jnp.where(at < vectors * comps, c // 32 * comps + lax.rem(at, comps), -1)

    def corner_lane(c):
        corner = c // 32
        at = lax.rem(c, 32)
        block = corner * 2 + jnp.where(corner >= 2, 2, 0)
        return jnp.where(at < vectors * comps, block * vectors + at // comps, -1)

    chosen = picked(part, lambda r: lax.rem(r, c_padded), corner_row, c_padded)
    blocks += folded(chosen, corner_lane)
    for k in range(9):
        blocks_out[0, 0, k] = blocks[:, k * vectors : (k + 1) * vectors]

    coarse_rhs = wave_sum(0)
    pltpu.make_async_copy(
        factors.at[pl.ds(0, n - 1)], factors.at[pl.ds(0, n - 1)], wave_recv.at[2]
    ).wait()

    def solve(vector):
        def one(d, total):
            f = factors[d]
            return total + f * jnp.sum(f * vector, axis=1, keepdims=True)

        zeros = jnp.zeros((factor.shape[0], order), F32)
        total = lax.fori_loop(0, n, one, zeros, unroll=n <= 32)
        return jnp.sum(total, axis=0, keepdims=True)

    first = solve(coarse_rhs)
    near = [
        iota((vectors, order), 1) == listing[0, 0, k] * vectors + iota((vectors, order), 0)
        for k in range(9)
    ]
    spread = jnp.concatenate([m.astype(F32) for m in near], axis=0)
    matrix_rows = jnp.dot(blocks, spread, preferred_element_type=F32, precision=HIGHEST)
    message[1] = placed(jnp.sum(matrix_rows * first, axis=1, keepdims=True))
    wave(1)

    for j in range(comps):
        for x in range(nx):
            store(ext, load(r32, pl.ds(j * cells + x * ny, ny)), j, 1 + x, pl.ds(1, ny))
    for side in range(2):
        at_x = side * (nx + 1)
        values = recv_x[side, pl.ds(vectors * x_rows, 32), :].astype(F32)
        for j in range(comps):
            store(ext, values[j * ny : (j + 1) * ny], j, at_x, pl.ds(1, ny))
        at_y = side * (ny + 1)
        values = recv_y[side, pl.ds(vectors * y_rows, 16), :].astype(F32)
        for j in range(comps):
            for x in range(nx):
                store(ext, values[j * nx + x : j * nx + x + 1], j, 1 + x, pl.ds(at_y, 1))
        for side_y in range(2):
            values = recv_c[side * 2 + side_y].astype(F32)
            for j in range(comps):
                at = vectors * comps + j
                store(ext, values[at : at + 1], j, at_x, pl.ds(side_y * (ny + 1), 1))

    half_x = (nx + 2) // 2
    half_y = (ny + 2) // 2
    kept_y = []
    for t in range(2):
        f = 2 * iota((half_y, depth), 0) + t
        kept_y.append((f >= margins[0, 0, 1, 0]) & (f < margins[0, 0, 1, 1]))
    inverse_copy.wait()
    for u in range(half_x):
        grouped = []
        for j in range(comps):
            for s in range(2):
                e = 2 * u + s
                kept = (e >= margins[0, 0, 0, 0]) & (e < margins[0, 0, 0, 1])
                factor_x = jnp.where(kept, 1.0, 0.0).astype(F32)
                for t in range(2):
                    values = load(ext, j, e, pl.ds(t, half_y, stride=2))
                    grouped.append(jnp.where(kept_y[t], values, 0.0) * factor_x)
        for j in range(comps):
            for s in range(2):
                x = 2 * u + s - 1
                if x < 0 or x >= nx:
                    continue
                for t in range(2):
                    i = 4 * j + 2 * s + t
                    acc = inverse[i, 0, u].astype(F32) * grouped[0]
                    for m in range(1, 4 * comps):
                        acc += inverse[i, m, u].astype(F32) * grouped[m]
                    store(loc, acc, j, x, pl.ds(t, half_y, stride=2))

    coarse_image = wave_sum(1)
    refined = first + solve(coarse_rhs - coarse_image)
    solution_out[...] = refined
    weights = jnp.sum(jnp.where(own_place, refined, 0.0), axis=1, keepdims=True)
    for j in range(comps):
        for x in range(nx):
            value = load(loc, j, x, pl.ds(1, ny))
            for a in range(vectors):
                at = (a * comps + j) * cells + x * ny
                value += weights[a : a + 1, :] * load(d32, pl.ds(at, ny))
            out[j, x] = value

    for number in range(2):
        pltpu.make_async_copy(slots.at[number], slots.at[number], wave_send.at[number]).wait()
    pltpu.make_async_copy(
        factors.at[pl.ds(0, n - 1)], factors.at[pl.ds(0, n - 1)], wave_send.at[2]
    ).wait()


def body(
    narrow,
    wide,
    deflation,
    residual,
    stiffness,
    mass,
    stencil,
    local_inverse,
    inverse_factor,
    margin_range,
    neighbor_blocks,
):
    vectors, comps, nx, ny, depth = deflation.shape
    n = narrow * wide
    order = inverse_factor.shape[1]
    cells = nx * ny
    places = stencil_places(comps, nx, ny)
    coupling = stencil.reshape(9, 3, comps, comps).transpose(3, 0, 1, 2)
    coupling = jnp.broadcast_to(
        coupling.reshape(comps * 9, 3 * comps, 1), (comps * 9, 3 * comps, cells)
    ).reshape(comps * 9, 3 * comps * cells)
    x_send = vectors * comps * ny + 32
    y_send = vectors * comps * nx + 16
    vmem = pl.BlockSpec(memory_space=pltpu.VMEM)
    smem = pl.BlockSpec(memory_space=pltpu.SMEM)
    result, blocks, refined = pl.pallas_call(
        functools.partial(kernel, narrow, wide, vectors, comps, nx, ny, depth),
        out_shape=(
            jax.ShapeDtypeStruct(residual.shape, F32),
            jax.ShapeDtypeStruct((1, 1, 9, vectors, vectors), F32),
            jax.ShapeDtypeStruct((1, order), F32),
        ),
        in_specs=[vmem] * 6 + [pl.BlockSpec(memory_space=pl.ANY), vmem, smem, smem],
        out_specs=(vmem, vmem, vmem),
        scratch_shapes=[
            pltpu.VMEM(local_inverse.shape, BF16),
            pltpu.VMEM((depth // 128, vectors * comps * cells, 128), F32),
            pltpu.VMEM((depth // 128, comps * cells, 128), F32),
            pltpu.VMEM((vectors, places.shape[0], depth), F32),
            pltpu.VMEM(places.shape, F32),
            pltpu.VMEM((2, 2, 3 * comps * cells, depth), BF16),
            pltpu.VMEM((32, depth), F32),
            pltpu.VMEM((depth // 128, comps, nx + 2, ny + 2, 128), F32),
            pltpu.VMEM((depth // 128, comps, nx, ny + 2, 128), F32),
            pltpu.VMEM((2, x_send, depth), BF16),
            pltpu.VMEM((2, y_send, depth), BF16),
            pltpu.VMEM((4, 32, depth), BF16),
            pltpu.VMEM((2, x_send, depth), BF16),
            pltpu.VMEM((2, y_send, depth), BF16),
            pltpu.VMEM((4, 32, depth), BF16),
            pltpu.VMEM((n,) + inverse_factor.shape, F32),
            pltpu.VMEM((2, 1, order), F32),
            pltpu.VMEM((2, n - 1, 1, order), F32),
            pltpu.SemaphoreType.DMA,
            pltpu.SemaphoreType.DMA((8,)),
            pltpu.SemaphoreType.DMA((8,)),
            pltpu.SemaphoreType.DMA((3,)),
            pltpu.SemaphoreType.DMA((3,)),
        ],
        compiler_params=pltpu.CompilerParams(
            collective_id=0, has_side_effects=True, vmem_limit_bytes=48 * 1024 * 1024
        ),
    )(
        deflation,
        residual,
        stiffness,
        mass,
        jnp.asarray(places),
        coupling,
        local_inverse,
        inverse_factor,
        margin_range,
        neighbor_blocks,
    )
    return result, blocks, refined.reshape(order)


def solution(mesh):
    placed = (
        P(None, None, "narrow", "wide", None),
        P(None, "narrow", "wide", None),
        P("narrow", "wide", None),
        P("narrow", "wide", None),
        P(),
        P(None, None, "narrow", "wide", None),
        P(("narrow", "wide"), None),
        P("narrow", "wide", None, None),
        P("narrow", "wide", None),
    )
    return jax.shard_map(
        functools.partial(body, mesh.shape["narrow"], mesh.shape["wide"]),
        mesh=mesh,
        in_specs=placed,
        out_specs=(P(None, "narrow", "wide", None), P("narrow", "wide", None, None, None), P()),
        check_vma=False,
    )
```

time: 443 us -> 29.7 us (0.07); the launches traced: 437 us -> 29.5 us
  blocking collectives: 164 us -> 0 us
  matrix products: 153 us -> 0 us
  local copies, waits for them, and re-layouts: 82.4 us -> 5.26 us
  Pallas kernels: 0 us -> 23.5 us
  starting transfers between devices: 21.4 us -> 0 us
  other arithmetic: 13.8 us -> 0 us
    psum x4 -> x0, blocking collectives: 164 us -> none  [the longest x2 81.8 us: solve(): return lax.psum(share, ('narrow', 'wide'))]
    dot_general x78 -> x0, matrix products: 153 us -> none  [the longest x27 87.9 us: coarse_blocks_of(): jnp.einsum('aixyz,bjxyz->aibjxy', weighted, piece.astype(jnp.float32), pr...]
    transpose x25 -> x1, local copies, waits for them, and re-layouts: 58.2 us -> 0.16 us  [body(): coupling = stencil.reshape(9, 3, comps, comps).transpose(3, 0, 1, 2)]
    pallas_call x0 -> x1, Pallas kernels: none -> 23.5 us  [body(): pl.pallas_call(functools.partial(kernel, narrow, wide, vectors, comps, nx...]
    ppermute x8 -> x0, starting transfers between devices: 21.4 us -> none  [the longest x4 16.2 us: extended_2(): lax.ppermute(lax.slice_in_dim(block, block.shape[dim] - width, None, axis...]
    squeeze x24 -> x0, local copies, waits for them, and re-layouts: 12.5 us -> none  [coarse_blocks_of(): stencil[offset]]
    slice x9 -> x0, local copies, waits for them, and re-layouts: 5.3 us -> none  [the longest x2 2.79 us: coarse_blocks_of(): stencil[offset]]
  transfers between devices with their start and end apart: 8 -> 0, of which waited for: 0 -> 0; matrix products, arithmetic and copies ran while one was open for 12% -> 0% of each run, Pallas kernels for 0% -> 0%
where the time goes in v1:
time: 29.7 us; the launch traced here: 29.5 us
  Pallas kernels  23.5 us (79%)
  local copies, waits for them, and re-layouts  5.26 us (18%)
  between operations  0.79 us (3%)
    pallas_call x1, Pallas kernels, body(): pl.pallas_call(functools.partial(kernel, narrow, wide, vectors, comps, nx...  23.5 us
    unnamed x20, local copies, waits for them, and re-layouts  3.93 us
    reshape x1, local copies, waits for them, and re-layouts, body(): coupling = stencil.reshape(9, 3, comps, comps).transpose(3, 0, 1, 2)  0.78 us

profile of v1, /device:TPU:0, one launch (start us, length us, event | category | flops | bytes accessed | tf_op | source)
XLA Modules:
  0.0 29.5 jit_solution(6273807412726040973)
XLA Ops:
  0.6 0.8 %reshape.17 = f32[9,3,3,3]{1,0,3,2:T(8,128)S(1)} reshape(f32[27,3,3]{0,2,1:T(4,128)} %param.14) | data formatting | bytes 1944 | tf_op jit(solution)/shard_map/reshape | solution.py:485
  1.4 0.2 copy.15
  1.6 0.1 broadcast_in_dim.7
  1.7 0.1 copy.16
  1.8 0.1 broadcast_in_dim.8
  1.9 0.0 copy-start
  1.9 0.0 copy-start.1
  1.9 0.0 copy-start.2
  1.9 0.0 copy-start.3
  1.9 0.0 copy-start.4
  1.9 0.0 copy-start.5
  1.9 0.0 copy-start.6
  2.0 0.0 copy-start.7
  2.0 0.1 reshape.18.coupling
  2.1 1.9 %copy.17.inverse_hbm = bf16[12,12,3,5,256]{4,3,2,1,0:T(8,128)(2,1)S(1)} copy(bf16[12,12,3,5,256]{4,2,3,1,0:T(4,128)(2,1)} %param.15) | data formatting | bytes 2211840 | tf_op args[5]
  4.0 0.0 copy-done
  4.0 0.0 copy-done.1
  4.0 0.0 copy-done.2
  4.1 0.0 copy-done.3
  4.1 0.0 copy-done.4
  4.1 23.5 %shard_map.121 = (f32[3,4,8,256]{3,2,1,0:T(8,128)S(1)}, f32[1,1,9,8,8]{4,3,2,1,0:T(8,128)S(1)}, f32[1,256]{1,0:T(1,128)S(1)}) custom-call(bf16[8,3,4,8,256]{4,3,2,1,0:T(8,128)(2,1)S(1)} %copy-done, f32[3,4,8,256]{3,2,1,0:T(8,128)S(1)} %copy-done.2, f32[4,8,256]{2,1,0:T(8,128)S(1)} %copy-done.3, f32[4,8,256]{2,1,0:T(8,128)S(1)} %copy-done.4, ...), custom_call_target="tpu_custom_call" | custom-call | tf_op jit(solution)/shard_map/pallas_call | solution.py:493
  27.6 0.7 %copy.18 = f32[1,1,9,8,8]{2,4,3,1,0:T(8,128)} copy(f32[1,1,9,8,8]{4,3,2,1,0:T(8,128)S(1)} %get-tuple-element.13) | data formatting | bytes 4608
  28.3 0.6 %copy.21 = f32[3,4,8,256]{3,2,1,0:T(8,128)} copy(f32[3,4,8,256]{3,2,1,0:T(8,128)S(1)} %get-tuple-element.18) | data formatting | bytes 196608
  29.0 0.6 %copy.22 = f32[256]{0:T(256)} copy(f32[256]{0:T(256)S(1)} %bitcast.6) | data formatting | bytes 2048
  (3 shorter events, 0.0 us)
Async XLA Ops:
  1.9 2.1 %copy-start = (bf16[8,3,4,8,256]{4,3,2,1,0:T(8,128)(2,1)S(1)}, bf16[8,3,4,8,256]{4,3,2,1,0:T(8,128)(2,1)}, u32[]{:S(2)}) copy-start(bf16[8,3,4,8,256]{4,3,2,1,0:T(8,128)(2,1)} %deflation.1) | copy-start | bytes 1179652
  1.9 2.1 %copy-start.1 = (s32[192,288]{1,0:T(8,128)S(1)}, s32[192,288]{1,0:T(8,128)}, u32[]{:S(2)}) copy-start(s32[192,288]{1,0:T(8,128)} %constant.2.clone.places) | copy-start | bytes 663556
  1.9 2.1 %copy-start.2 = (f32[3,4,8,256]{3,2,1,0:T(8,128)S(1)}, f32[3,4,8,256]{3,2,1,0:T(8,128)}, u32[]{:S(2)}) copy-start(f32[3,4,8,256]{3,2,1,0:T(8,128)} %residual.1) | copy-start | bytes 294916
  1.9 2.1 %copy-start.3 = (f32[4,8,256]{2,1,0:T(8,128)S(1)}, f32[4,8,256]{2,1,0:T(8,128)}, u32[]{:S(2)}) copy-start(f32[4,8,256]{2,1,0:T(8,128)} %stiffness.1) | copy-start | bytes 98308
  1.9 2.1 %copy-start.4 = (f32[4,8,256]{2,1,0:T(8,128)S(1)}, f32[4,8,256]{2,1,0:T(8,128)}, u32[]{:S(2)}) copy-start(f32[4,8,256]{2,1,0:T(8,128)} %mass.1) | copy-start | bytes 98308
  1.9 2.1 %copy-start.5 = (f32[8,256]{1,0:T(8,128)S(1)}, f32[8,256]{1,0:T(8,128)}, u32[]{:S(2)}) copy-start(f32[8,256]{1,0:T(8,128)} %factor.1) | copy-start | bytes 24580
  1.9 2.1 %copy-start.6 = (s32[1,1,2,2]{3,2,1,0:T(2,128)S(1)}, s32[1,1,2,2]{3,2,1,0:T(2,128)}, u32[]{:S(2)}) copy-start(s32[1,1,2,2]{3,2,1,0:T(2,128)} %margins.1) | copy-start | bytes 52
  2.0 2.1 %copy-start.7 = (s32[1,1,9]{2,1,0:T(1,128)S(1)}, s32[1,1,9]{2,1,0:T(1,128)}, u32[]{:S(2)}) copy-start(s32[1,1,9]{2,1,0:T(1,128)} %listing.1) | copy-start | bytes 112

commit v2 on v1

--- a/solution.py
+++ b/solution.py
@@ -64,6 +64,10 @@
         ref[(h,) + at] = values[:, h * 128 : (h + 1) * 128]
 
 
+def quotient(values, size, count):
+    return sum((values >= k * size).astype(jnp.int32) for k in range(1, count))
+
+
 def gram(left, right):
     dims = (((1,), (1,)), ((), ()))
     high, low = split(left)
@@ -85,7 +89,7 @@
     stiffness,
     mass,
     places,
-    coupling,
+    stencil,
     inverse_hbm,
     factor,
     margins,
@@ -125,17 +129,32 @@
     cells = nx * ny
     own_rows = comps * cells
 
-    def target_of(k):
-        t = lax.rem(me + k, n)
-        return (t // wide, lax.rem(t, wide))
-
+    def turned(here, count):
+        places_of = [here + k for k in range(count)]
+        return [jnp.where(at >= count, at - count, at) for at in places_of]
+
+    target_rows = turned(row, narrow)
+
+    def to_others(act):
+        if n <= 64:
+            for k in range(1, n):
+                act(k - 1, (target_rows[k // wide], target_columns[k % wide]))
+            return
+
+        def one(k, carry):
+            t = lax.rem(me + k, n)
+            act(k - 1, (t // wide, lax.rem(t, wide)))
+            return carry
+
+        lax.fori_loop(1, n, one, 0)
+
+    target_columns = turned(column, wide) if n <= 64 else None
     barrier = pltpu.get_barrier_semaphore()
 
-    def greet(k, carry):
-        pl.semaphore_signal(barrier, inc=1, device_id=target_of(k), device_id_type=MESH)
-        return carry
-
-    lax.fori_loop(1, n, greet, 0)
+    def greet(k, device):
+        pl.semaphore_signal(barrier, inc=1, device_id=device, device_id_type=MESH)
+
+    to_others(greet)
 
     inverse_copy = pltpu.make_async_copy(inverse_hbm, inverse, inverse_sem)
     inverse_copy.start()
@@ -183,21 +202,44 @@
             stage[pl.ds(vectors * comps, comps), :] = load(r32, pl.ds(at, comps, stride=cells))
             send_c[side_x * 2 + side_y] = stage[...].astype(BF16)
 
+    total_rows = places.shape[0]
+    fixed = own_rows + 2 * x_rows
+    group = quotient(iota((1, 3 * own_rows), 1), cells, 3 * comps)
+    lanes_of = [group == g for g in range(3 * comps)]
+    coupling = []
+    for j in range(comps):
+        for d in range(9):
+            line = jnp.zeros((1, 3 * own_rows), F32)
+            for oz in range(3):
+                for i in range(comps):
+                    line = jnp.where(lanes_of[oz * comps + i], stencil[i, j, d * 3 + oz], line)
+            coupling.append(line)
+    chunks = [(j * cells, cells, j) for j in range(comps)]
+    for side in range(2):
+        chunks += [(own_rows + side * x_rows + j * ny, ny, j) for j in range(comps)]
+    chunks.append((fixed, total_rows - fixed, None))
+    for start, size, j in chunks:
+        here = places[pl.ds(start, size), :]
+        value = jnp.zeros(here.shape, F32)
+        for e in range(comps * 9) if j is None else range(j * 9, j * 9 + 9):
+            value = jnp.where(here == e, coupling[e], value)
+        s_parts[pl.ds(start, size), :] = value
+    s_high, s_low = split(s_parts[...])
+
     pl.semaphore_wait(barrier, n - 1)
 
     def wave(number):
-        def one(k, carry):
+        def one(k, device):
             pltpu.make_async_remote_copy(
                 src_ref=message.at[number],
-                dst_ref=slots.at[number, k - 1],
+                dst_ref=slots.at[number, k],
                 send_sem=wave_send.at[number],
                 recv_sem=wave_recv.at[number],
-                device_id=target_of(k),
+                device_id=device,
                 device_id_type=MESH,
             ).start()
-            return carry
-
-        lax.fori_loop(1, n, one, 0)
+
+        to_others(one)
 
     def wave_sum(number):
         pltpu.make_async_copy(slots.at[number], slots.at[number], wave_recv.at[number]).wait()
@@ -248,32 +290,17 @@
 
     factors[me] = factor[...]
 
-    def send_factor(k, carry):
+    def send_factor(k, device):
         pltpu.make_async_remote_copy(
             src_ref=factor,
             dst_ref=factors.at[me],
             send_sem=wave_send.at[2],
             recv_sem=wave_recv.at[2],
-            device_id=target_of(k),
+            device_id=device,
             device_id_type=MESH,
         ).start()
-        return carry
-
-    lax.fori_loop(1, n, send_factor, 0)
-
-    total_rows = places.shape[0]
-    fixed = own_rows + 2 * x_rows
-    chunks = [(j * cells, cells, j) for j in range(comps)]
-    for side in range(2):
-        chunks += [(own_rows + side * x_rows + j * ny, ny, j) for j in range(comps)]
-    chunks.append((fixed, total_rows - fixed, None))
-    for start, size, j in chunks:
-        here = places[pl.ds(start, size), :]
-        value = jnp.zeros(here.shape, F32)
-        for e in range(comps * 9) if j is None else range(j * 9, j * 9 + 9):
-            value = jnp.where(here == e, coupling[pl.ds(e, 1), :], value)
-        s_parts[pl.ds(start, size), :] = value
-    s_high, s_low = split(s_parts[...])
+
+    to_others(send_factor)
 
     lane = iota((own_rows, depth), 1)
     scale = jnp.concatenate([stiffness[...].reshape(cells, depth)] * comps, axis=0)
@@ -299,16 +326,22 @@
 
     width = 9 * vectors
 
-    def picked(product, left_of, right_of, left_size):
-        r = iota(product.shape, 0)
-        c = iota(product.shape, 1)
-        kept = jnp.where(left_of(r) == right_of(c), product, 0.0)
-        return jnp.sum(kept.reshape(vectors, left_size, product.shape[1]), axis=1)
+    def picked(product, row_of, left_size):
+        columns = product.shape[1]
+        kept = iota((left_size, columns), 0) == row_of(iota((1, columns), 1))
+        parts = product.reshape(vectors, left_size, columns)
+        return jnp.sum(jnp.where(kept[None], parts, 0.0), axis=1)
 
     def folded(values, lane_of):
-        shape = (values.shape[1], width)
-        chosen = (lane_of(iota(shape, 0)) == iota(shape, 1)).astype(F32)
+        rows = values.shape[1]
+        chosen = (lane_of(iota((rows, 1), 0)) == iota((rows, width), 1)).astype(F32)
         return jnp.dot(values, chosen, preferred_element_type=F32, precision=HIGHEST)
+
+    def within(size):
+        return lambda c: c - size * quotient(c, size, vectors)
+
+    def lane_in(block, size):
+        return lambda c: block * vectors + quotient(c, size, vectors)
 
     total = None
     for j in range(comps):
@@ -318,8 +351,7 @@
         ).astype(BF16)
         part = gram(left, right)
         total = part if total is None else total + part
-    chosen = picked(total, lambda r: lax.rem(r, cells), lambda c: lax.rem(c, cells), cells)
-    blocks = folded(chosen, lambda c: 4 * vectors + c // cells)
+    blocks = folded(picked(total, within(cells), cells), lane_in(4, cells))
 
     for k, (source, target, landing, shift_x, shift_y) in enumerate(copies()):
 
@@ -339,39 +371,47 @@
             landing[...] = jnp.zeros(landing.shape, BF16)
 
     for side in range(2):
-        n_class = (1 if side == 0 else 7) * vectors
+        block = 1 if side == 0 else 7
         left = t32[:, pl.ds(own_rows + side * x_rows, x_rows), :].reshape(vectors * x_rows, depth)
         part = gram(left, recv_x[side, pl.ds(0, vectors * x_rows), :])
-        chosen = picked(part, lambda r: lax.rem(r, x_rows), lambda c: lax.rem(c, x_rows), x_rows)
-        blocks += folded(chosen, lambda c, at=n_class: at + c // x_rows)
+        blocks += folded(picked(part, within(x_rows), x_rows), lane_in(block, x_rows))
     y_padded = pad_to(y_rows, 8)
     for side in range(2):
-        n_class = (3 if side == 0 else 5) * vectors
+        block = 3 if side == 0 else 5
         left = t32[:, pl.ds(fixed + side * y_padded, y_padded), :]
         left = left.reshape(vectors * y_padded, depth)
         part = gram(left, recv_y[side, pl.ds(0, vectors * y_rows), :])
-        chosen = picked(
-            part, lambda r: lax.rem(r, y_padded), lambda c: lax.rem(c, y_rows), y_padded
-        )
-        blocks += folded(chosen, lambda c, at=n_class: at + c // y_rows)
+        blocks += folded(picked(part, within(y_rows), y_padded), lane_in(block, y_rows))
     c_padded = pad_to(4 * comps, 8)
     left = t32[:, pl.ds(fixed + 2 * y_padded, c_padded), :].reshape(vectors * c_padded, depth)
     part = gram(left, recv_c[...].reshape(4 * 32, depth))
 
+    def corner_parts(c):
+        corner = quotient(c, 32, 4)
+        at = c - 32 * corner
+        vector = quotient(at, comps, vectors)
+        return at < vectors * comps, corner, vector, at - comps * vector
+
     def corner_row(c):
-        at = lax.rem(c, 32)
-        return jnp.where(at < vectors * comps, c // 32 * comps + lax.rem(at, comps), -1)
+        real, corner, _, j = corner_parts(c)
+        return jnp.where(real, corner * comps + j, -1)
 
     def corner_lane(c):
-        corner = c // 32
-        at = lax.rem(c, 32)
+        real, corner, vector, _ = corner_parts(c)
         block = corner * 2 + jnp.where(corner >= 2, 2, 0)
-        return jnp.where(at < vectors * comps, block * vectors + at // comps, -1)
-
-    chosen = picked(part, lambda r: lax.rem(r, c_padded), corner_row, c_padded)
-    blocks += folded(chosen, corner_lane)
-    for k in range(9):
-        blocks_out[0, 0, k] = blocks[:, k * vectors : (k + 1) * vectors]
+        return jnp.where(real, block * vectors + vector, -1)
+
+    blocks += folded(picked(part, corner_row, c_padded), corner_lane)
+
+    pairs = vectors * vectors
+    repeated = jnp.broadcast_to(blocks[:, None, :], (vectors, vectors, width))
+    right = iota((1, vectors, width), 2)
+    right = right - vectors * quotient(right, vectors, 9)
+    kept = jnp.where(right == iota((1, vectors, width), 1), repeated, 0.0).reshape(pairs, width)
+    neighbour = quotient(iota((width, 1), 0), vectors, 9)
+    to_lane = (neighbour == iota((width, 9), 1)).astype(F32)
+    turned_blocks = jnp.dot(kept, to_lane, preferred_element_type=F32, precision=HIGHEST)
+    blocks_out[0, 0] = turned_blocks.reshape(vectors, vectors, 9)
 
     coarse_rhs = wave_sum(0)
     pltpu.make_async_copy(
@@ -397,53 +437,61 @@
     message[1] = placed(jnp.sum(matrix_rows * first, axis=1, keepdims=True))
     wave(1)
 
+    high_y = ny + 2
+
+    def ext_at(j, f, e):
+        return (j * high_y + f) * 8 + e
+
     for j in range(comps):
-        for x in range(nx):
-            store(ext, load(r32, pl.ds(j * cells + x * ny, ny)), j, 1 + x, pl.ds(1, ny))
+        for y in range(ny):
+            values = load(r32, pl.ds(j * cells + y, nx, stride=ny))
+            store(ext, values, pl.ds(ext_at(j, 1 + y, 1), nx))
     for side in range(2):
         at_x = side * (nx + 1)
         values = recv_x[side, pl.ds(vectors * x_rows, 32), :].astype(F32)
         for j in range(comps):
-            store(ext, values[j * ny : (j + 1) * ny], j, at_x, pl.ds(1, ny))
+            for y in range(ny):
+                line = values[j * ny + y : j * ny + y + 1]
+                store(ext, line, pl.ds(ext_at(j, 1 + y, at_x), 1))
         at_y = side * (ny + 1)
         values = recv_y[side, pl.ds(vectors * y_rows, 16), :].astype(F32)
         for j in range(comps):
-            for x in range(nx):
-                store(ext, values[j * nx + x : j * nx + x + 1], j, 1 + x, pl.ds(at_y, 1))
+            store(ext, values[j * nx : (j + 1) * nx], pl.ds(ext_at(j, at_y, 1), nx))
         for side_y in range(2):
             values = recv_c[side * 2 + side_y].astype(F32)
             for j in range(comps):
                 at = vectors * comps + j
-                store(ext, values[at : at + 1], j, at_x, pl.ds(side_y * (ny + 1), 1))
+                line = values[at : at + 1]
+                store(ext, line, pl.ds(ext_at(j, side_y * (ny + 1), at_x), 1))
 
     half_x = (nx + 2) // 2
     half_y = (ny + 2) // 2
-    kept_y = []
-    for t in range(2):
-        f = 2 * iota((half_y, depth), 0) + t
-        kept_y.append((f >= margins[0, 0, 1, 0]) & (f < margins[0, 0, 1, 1]))
+    kept_x = []
+    for s in range(2):
+        e = 2 * iota((half_x, depth), 0) + s
+        kept_x.append((e >= margins[0, 0, 0, 0]) & (e < margins[0, 0, 0, 1]))
     inverse_copy.wait()
-    for u in range(half_x):
+    for v in range(half_y):
         grouped = []
         for j in range(comps):
             for s in range(2):
-                e = 2 * u + s
-                kept = (e >= margins[0, 0, 0, 0]) & (e < margins[0, 0, 0, 1])
-                factor_x = jnp.where(kept, 1.0, 0.0).astype(F32)
                 for t in range(2):
-                    values = load(ext, j, e, pl.ds(t, half_y, stride=2))
-                    grouped.append(jnp.where(kept_y[t], values, 0.0) * factor_x)
+                    f = 2 * v + t
+                    kept = (f >= margins[0, 0, 1, 0]) & (f < margins[0, 0, 1, 1])
+                    factor_y = jnp.where(kept, 1.0, 0.0).astype(F32)
+                    values = load(ext, pl.ds(ext_at(j, f, s), half_x, stride=2))
+                    grouped.append(jnp.where(kept_x[s], values, 0.0) * factor_y)
         for j in range(comps):
             for s in range(2):
-                x = 2 * u + s - 1
-                if x < 0 or x >= nx:
-                    continue
                 for t in range(2):
+                    f = 2 * v + t
+                    if f == 0 or f == ny + 1:
+                        continue
                     i = 4 * j + 2 * s + t
-                    acc = inverse[i, 0, u].astype(F32) * grouped[0]
+                    acc = inverse[i, 0, v].astype(F32) * grouped[0]
                     for m in range(1, 4 * comps):
-                        acc += inverse[i, m, u].astype(F32) * grouped[m]
-                    store(loc, acc, j, x, pl.ds(t, half_y, stride=2))
+                        acc += inverse[i, m, v].astype(F32) * grouped[m]
+                    store(loc, acc, pl.ds(ext_at(j, f, s), half_x, stride=2))
 
     coarse_image = wave_sum(1)
     refined = first + solve(coarse_rhs - coarse_image)
@@ -451,7 +499,7 @@
     weights = jnp.sum(jnp.where(own_place, refined, 0.0), axis=1, keepdims=True)
     for j in range(comps):
         for x in range(nx):
-            value = load(loc, j, x, pl.ds(1, ny))
+            value = load(loc, pl.ds(ext_at(j, 1, 1 + x), ny, stride=8))
             for a in range(vectors):
                 at = (a * comps + j) * cells + x * ny
                 value += weights[a : a + 1, :] * load(d32, pl.ds(at, ny))
@@ -482,10 +530,7 @@
     order = inverse_factor.shape[1]
     cells = nx * ny
     places = stencil_places(comps, nx, ny)
-    coupling = stencil.reshape(9, 3, comps, comps).transpose(3, 0, 1, 2)
-    coupling = jnp.broadcast_to(
-        coupling.reshape(comps * 9, 3 * comps, 1), (comps * 9, 3 * comps, cells)
-    ).reshape(comps * 9, 3 * comps * cells)
+    turned_inverse = local_inverse.transpose(0, 1, 3, 2, 4)
     x_send = vectors * comps * ny + 32
     y_send = vectors * comps * nx + 16
     vmem = pl.BlockSpec(memory_space=pltpu.VMEM)
@@ -494,21 +539,21 @@
         functools.partial(kernel, narrow, wide, vectors, comps, nx, ny, depth),
         out_shape=(
             jax.ShapeDtypeStruct(residual.shape, F32),
-            jax.ShapeDtypeStruct((1, 1, 9, vectors, vectors), F32),
+            jax.ShapeDtypeStruct((1, 1, vectors, vectors, 9), F32),
             jax.ShapeDtypeStruct((1, order), F32),
         ),
-        in_specs=[vmem] * 6 + [pl.BlockSpec(memory_space=pl.ANY), vmem, smem, smem],
+        in_specs=[vmem] * 5 + [smem, pl.BlockSpec(memory_space=pl.ANY), vmem, smem, smem],
         out_specs=(vmem, vmem, vmem),
         scratch_shapes=[
-            pltpu.VMEM(local_inverse.shape, BF16),
+            pltpu.VMEM(turned_inverse.shape, BF16),
             pltpu.VMEM((depth // 128, vectors * comps * cells, 128), F32),
             pltpu.VMEM((depth // 128, comps * cells, 128), F32),
             pltpu.VMEM((vectors, places.shape[0], depth), F32),
             pltpu.VMEM(places.shape, F32),
             pltpu.VMEM((2, 2, 3 * comps * cells, depth), BF16),
             pltpu.VMEM((32, depth), F32),
-            pltpu.VMEM((depth // 128, comps, nx + 2, ny + 2, 128), F32),
-            pltpu.VMEM((depth // 128, comps, nx, ny + 2, 128), F32),
+            pltpu.VMEM((depth // 128, comps * (ny + 2) * 8, 128), F32),
+            pltpu.VMEM((depth // 128, comps * (ny + 2) * 8, 128), F32),
             pltpu.VMEM((2, x_send, depth), BF16),
             pltpu.VMEM((2, y_send, depth), BF16),
             pltpu.VMEM((4, 32, depth), BF16),
@@ -525,7 +570,7 @@
             pltpu.SemaphoreType.DMA((3,)),
         ],
         compiler_params=pltpu.CompilerParams(
-            collective_id=0, has_side_effects=True, vmem_limit_bytes=48 * 1024 * 1024
+            collective_id=0, has_side_effects=True, vmem_limit_bytes=60 * 1024 * 1024
         ),
     )(
         deflation,
@@ -533,13 +578,13 @@
         stiffness,
         mass,
         jnp.asarray(places),
-        coupling,
-        local_inverse,
+        stencil.transpose(1, 2, 0),
+        turned_inverse,
         inverse_factor,
         margin_range,
         neighbor_blocks,
     )
-    return result, blocks, refined.reshape(order)
+    return result, blocks.transpose(0, 1, 4, 2, 3), refined.reshape(order)
 
 
 def solution(mesh):

time: 29.7 us -> 29.6 us (level)
  local copies, waits for them, and re-layouts: 5.26 us -> 4.14 us
  Pallas kernels: 23.5 us -> 24.6 us
    pallas_call x1, Pallas kernels: 23.5 us -> 24.6 us  [body(): pl.pallas_call(functools.partial(kernel, narrow, wide, vectors, comps, nx...]
    reshape x2 -> x0, local copies, waits for them, and re-layouts: 0.88 us -> none  [the longest x1 0.78 us: body(): coupling = stencil.reshape(9, 3, comps, comps).transpose(3, 0, 1, 2)]
    unnamed x20 -> x3, local copies, waits for them, and re-layouts: 3.93 us -> 4.14 us
where the time goes in v2:
time: 29.6 us; the launch traced here: 29.4 us
  Pallas kernels  24.6 us (83%)
  local copies, waits for them, and re-layouts  4.14 us (14%)
  between operations  0.64 us (2%)
    pallas_call x1, Pallas kernels, body(): pl.pallas_call(functools.partial(kernel, narrow, wide, vectors, comps, nx...  24.6 us
    unnamed x3, local copies, waits for them, and re-layouts  4.14 us

profile of v2, /device:TPU:0, one launch (start us, length us, event | category | flops | bytes accessed | tf_op | source)
XLA Modules:
  0.0 29.4 jit_solution(3973722659648238769)
XLA Ops:
  0.6 24.6 %shard_map.121 = (f32[3,4,8,256]{3,2,1,0:T(8,128)}, f32[1,1,8,8,9]{4,3,2,1,0:T(8,128)}, f32[1,256]{1,0:T(1,128)}) custom-call(bf16[8,3,4,8,256]{4,3,2,1,0:T(8,128)(2,1)} %deflation.1, f32[3,4,8,256]{3,2,1,0:T(8,128)} %residual.1, f32[4,8,256]{2,1,0:T(8,128)} %stiffness.1, f32[4,8,256]{2,1,0:T(8,128)} %mass.1, s32[192,288]{1,0:T(8,128)} %constant.2.clone.places, ...), custom_call_target="tpu_custom_call" | custom-call | tf_op jit(solution)/shard_map/pallas_call | solution.py:538
  25.2 1.5 %copy.16 = f32[3,4,8,256]{3,2,1,0:T(8,128)} copy(f32[3,4,8,256]{3,2,1,0:T(8,128)} %get-tuple-element.12) | data formatting | bytes 196608
  26.8 1.4 %copy.17 = f32[1,1,9,8,8]{2,4,3,1,0:T(8,128)} copy(f32[1,1,9,8,8]{2,4,3,1,0:T(8,128)} %bitcast.5) | data formatting | bytes 4608
  28.2 1.2 %copy.18 = f32[256]{0:T(256)} copy(f32[256]{0:T(256)} %bitcast.7) | data formatting | bytes 2048

commit v3 on v2

--- a/solution.py
+++ b/solution.py
@@ -102,7 +102,6 @@
     r32,
     t32,
     s_parts,
-    w_parts,
     stage,
     ext,
     loc,
@@ -135,20 +134,11 @@
 
     target_rows = turned(row, narrow)
 
-    def to_others(act):
-        if n <= 64:
-            for k in range(1, n):
-                act(k - 1, (target_rows[k // wide], target_columns[k % wide]))
-            return
-
-        def one(k, carry):
-            t = lax.rem(me + k, n)
-            act(k - 1, (t // wide, lax.rem(t, wide)))
-            return carry
-
-        lax.fori_loop(1, n, one, 0)
-
-    target_columns = turned(column, wide) if n <= 64 else None
+    target_columns = turned(column, wide)
+
+    def to_others(act, step=1):
+        for k in range(step, n, step):
+            act(k // step - 1, (target_rows[k // wide], target_columns[k % wide]))
     barrier = pltpu.get_barrier_semaphore()
 
     def greet(k, device):
@@ -161,12 +151,18 @@
 
     rounded = residual[...].astype(BF16).astype(F32).reshape(own_rows, depth)
     store(r32, rounded, pl.ds(0, own_rows))
-    sums = []
-    for a in range(vectors):
+
+    def rows_of(a):
+        return pl.ds(pl.multiple_of(a * own_rows, own_rows), own_rows)
+
+    def widen(a, carry):
         d = deflation[a].astype(F32).reshape(own_rows, depth)
-        store(d32, d, pl.ds(a * own_rows, own_rows))
-        sums.append(jnp.sum(d * rounded, axis=0, keepdims=True))
-    rhs_column = jnp.sum(jnp.concatenate(sums, axis=0), axis=1, keepdims=True)
+        store(d32, d, rows_of(a))
+        stage[pl.ds(a, 1), :] = jnp.sum(d * rounded, axis=0, keepdims=True)
+        return carry
+
+    lax.fori_loop(0, vectors, widen, 0, unroll=2)
+    rhs_column = jnp.sum(stage[pl.ds(0, vectors), :], axis=1, keepdims=True)
     own_block = listing[0, 0, 4]
     own_place = iota((vectors, order), 1) == own_block * vectors + iota((vectors, order), 0)
 
@@ -288,41 +284,61 @@
         def _(k=k, source=source, target=target, shift_x=shift_x, shift_y=shift_y):
             face_copy(k, source, target, shift_x, shift_y).start()
 
-    factors[me] = factor[...]
+    parity = lax.rem(column, 2)
+    half_index = row * (wide // 2) + column // 2
+    partner = (row, column + 1 - 2 * parity)
+    factors[parity, half_index] = factor[...]
 
     def send_factor(k, device):
         pltpu.make_async_remote_copy(
             src_ref=factor,
-            dst_ref=factors.at[me],
+            dst_ref=factors.at[parity, half_index],
             send_sem=wave_send.at[2],
             recv_sem=wave_recv.at[2],
             device_id=device,
             device_id_type=MESH,
         ).start()
 
-    to_others(send_factor)
+    to_others(send_factor, 2)
+
+    def others_rows():
+        some = factors.at[0, pl.ds(0, n // 2 - 1)]
+        return some, some
 
     lane = iota((own_rows, depth), 1)
     scale = jnp.concatenate([stiffness[...].reshape(cells, depth)] * comps, axis=0)
     weight = jnp.concatenate([mass[...].reshape(cells, depth)] * comps, axis=0)
-    for a in range(vectors):
-        d = load(d32, pl.ds(a * own_rows, own_rows))
+
+    def adjoint(a, carry):
+        d = load(d32, rows_of(a))
         w = d * scale
         before = jnp.where(lane == depth - 1, 0.0, pltpu.roll(w, depth - 1, axis=1))
         after = jnp.where(lane == 0, 0.0, pltpu.roll(w, 1, axis=1))
-        for oz, shifted in enumerate((before, w, after)):
-            high, low = split(shifted)
-            w_parts[a % 2, 0, pl.ds(oz * own_rows, own_rows), :] = high
-            w_parts[a % 2, 1, pl.ds(oz * own_rows, own_rows), :] = low
-        high = w_parts[a % 2, 0]
-        low = w_parts[a % 2, 1]
+        parts = [split(shifted) for shifted in (before, w, after)]
+        high = jnp.concatenate([part[0] for part in parts], axis=0)
+        low = jnp.concatenate([part[1] for part in parts], axis=0)
         image = (
             jnp.dot(s_high, high, preferred_element_type=F32)
             + jnp.dot(s_high, low, preferred_element_type=F32)
             + jnp.dot(s_low, high, preferred_element_type=F32)
         )
-        t32[a] = image
+        t32[a, pl.ds(own_rows, total_rows - own_rows), :] = image[own_rows:]
         t32[a, pl.ds(0, own_rows), :] = image[:own_rows] + weight * d
+        return carry
+
+    lax.fori_loop(0, vectors, adjoint, 0, unroll=2)
+
+    some, same = others_rows()
+    pltpu.make_async_copy(some, same, wave_recv.at[2]).wait()
+    hand_on = pltpu.make_async_remote_copy(
+        src_ref=factors.at[parity],
+        dst_ref=factors.at[parity],
+        send_sem=wave_send.at[3],
+        recv_sem=wave_recv.at[3],
+        device_id=partner,
+        device_id_type=MESH,
+    )
+    hand_on.start()
 
     width = 9 * vectors
 
@@ -414,17 +430,17 @@
     blocks_out[0, 0] = turned_blocks.reshape(vectors, vectors, 9)
 
     coarse_rhs = wave_sum(0)
-    pltpu.make_async_copy(
-        factors.at[pl.ds(0, n - 1)], factors.at[pl.ds(0, n - 1)], wave_recv.at[2]
-    ).wait()
+    hand_on.wait()
 
     def solve(vector):
         def one(d, total):
-            f = factors[d]
-            return total + f * jnp.sum(f * vector, axis=1, keepdims=True)
+            for half in range(2):
+                f = factors[half, d]
+                total = total + f * jnp.sum(f * vector, axis=1, keepdims=True)
+            return total
 
         zeros = jnp.zeros((factor.shape[0], order), F32)
-        total = lax.fori_loop(0, n, one, zeros, unroll=n <= 32)
+        total = lax.fori_loop(0, n // 2, one, zeros, unroll=8)
         return jnp.sum(total, axis=0, keepdims=True)
 
     first = solve(coarse_rhs)
@@ -471,7 +487,8 @@
         e = 2 * iota((half_x, depth), 0) + s
         kept_x.append((e >= margins[0, 0, 0, 0]) & (e < margins[0, 0, 0, 1]))
     inverse_copy.wait()
-    for v in range(half_y):
+
+    def local_row(v, carry):
         grouped = []
         for j in range(comps):
             for s in range(2):
@@ -484,14 +501,14 @@
         for j in range(comps):
             for s in range(2):
                 for t in range(2):
-                    f = 2 * v + t
-                    if f == 0 or f == ny + 1:
-                        continue
                     i = 4 * j + 2 * s + t
                     acc = inverse[i, 0, v].astype(F32) * grouped[0]
                     for m in range(1, 4 * comps):
                         acc += inverse[i, m, v].astype(F32) * grouped[m]
-                    store(loc, acc, pl.ds(ext_at(j, f, s), half_x, stride=2))
+                    store(loc, acc, pl.ds(ext_at(j, 2 * v + t, s), half_x, stride=2))
+        return carry
+
+    lax.fori_loop(0, half_y, local_row, 0)
 
     coarse_image = wave_sum(1)
     refined = first + solve(coarse_rhs - coarse_image)
@@ -507,9 +524,19 @@
 
     for number in range(2):
         pltpu.make_async_copy(slots.at[number], slots.at[number], wave_send.at[number]).wait()
-    pltpu.make_async_copy(
-        factors.at[pl.ds(0, n - 1)], factors.at[pl.ds(0, n - 1)], wave_send.at[2]
-    ).wait()
+    pltpu.make_async_copy(some, same, wave_send.at[2]).wait()
+
+
+def write_out(*refs):
+    sources, targets, sems = refs[:3], refs[3:6], refs[6]
+    copies = [
+        pltpu.make_async_copy(source, target, sems.at[k])
+        for k, (source, target) in enumerate(zip(sources, targets))
+    ]
+    for copy in copies:
+        copy.start()
+    for copy in copies:
+        copy.wait()
 
 
 def body(
@@ -535,14 +562,14 @@
     y_send = vectors * comps * nx + 16
     vmem = pl.BlockSpec(memory_space=pltpu.VMEM)
     smem = pl.BlockSpec(memory_space=pltpu.SMEM)
-    result, blocks, refined = pl.pallas_call(
+    results = pl.pallas_call(
         functools.partial(kernel, narrow, wide, vectors, comps, nx, ny, depth),
         out_shape=(
             jax.ShapeDtypeStruct(residual.shape, F32),
             jax.ShapeDtypeStruct((1, 1, vectors, vectors, 9), F32),
             jax.ShapeDtypeStruct((1, order), F32),
         ),
-        in_specs=[vmem] * 5 + [smem, pl.BlockSpec(memory_space=pl.ANY), vmem, smem, smem],
+        in_specs=[vmem] * 5 + [smem, pl.BlockSpec(memory_space=pltpu.HBM), vmem, smem, smem],
         out_specs=(vmem, vmem, vmem),
         scratch_shapes=[
             pltpu.VMEM(turned_inverse.shape, BF16),
@@ -550,7 +577,6 @@
             pltpu.VMEM((depth // 128, comps * cells, 128), F32),
             pltpu.VMEM((vectors, places.shape[0], depth), F32),
             pltpu.VMEM(places.shape, F32),
-            pltpu.VMEM((2, 2, 3 * comps * cells, depth), BF16),
             pltpu.VMEM((32, depth), F32),
             pltpu.VMEM((depth // 128, comps * (ny + 2) * 8, 128), F32),
             pltpu.VMEM((depth // 128, comps * (ny + 2) * 8, 128), F32),
@@ -560,17 +586,17 @@
             pltpu.VMEM((2, x_send, depth), BF16),
             pltpu.VMEM((2, y_send, depth), BF16),
             pltpu.VMEM((4, 32, depth), BF16),
-            pltpu.VMEM((n,) + inverse_factor.shape, F32),
+            pltpu.VMEM((2, n // 2) + inverse_factor.shape, F32),
             pltpu.VMEM((2, 1, order), F32),
             pltpu.VMEM((2, n - 1, 1, order), F32),
             pltpu.SemaphoreType.DMA,
             pltpu.SemaphoreType.DMA((8,)),
             pltpu.SemaphoreType.DMA((8,)),
-            pltpu.SemaphoreType.DMA((3,)),
-            pltpu.SemaphoreType.DMA((3,)),
+            pltpu.SemaphoreType.DMA((4,)),
+            pltpu.SemaphoreType.DMA((4,)),
         ],
         compiler_params=pltpu.CompilerParams(
-            collective_id=0, has_side_effects=True, vmem_limit_bytes=60 * 1024 * 1024
+            collective_id=0, has_side_effects=True, vmem_limit_bytes=40 * 1024 * 1024
         ),
     )(
         deflation,
@@ -584,6 +610,13 @@
         margin_range,
         neighbor_blocks,
     )
+    result, blocks, refined = pl.pallas_call(
+        write_out,
+        out_shape=tuple(jax.ShapeDtypeStruct(r.shape, r.dtype) for r in results),
+        in_specs=[vmem] * 3,
+        out_specs=tuple(pl.BlockSpec(memory_space=pltpu.HBM) for _ in results),
+        scratch_shapes=[pltpu.SemaphoreType.DMA((3,))],
+    )(*results)
     return result, blocks.transpose(0, 1, 4, 2, 3), refined.reshape(order)
 
 

time: 29.6 us -> 36.8 us (1.24)
  local copies, waits for them, and re-layouts: 4.14 us -> 10.2 us
  Pallas kernels: 24.6 us -> 25.4 us
    unnamed x3 -> x26, local copies, waits for them, and re-layouts: 4.14 us -> 10.2 us
    pallas_call x0 -> x1, Pallas kernels: none -> 1.59 us  [body(): pl.pallas_call(write_out, out_shape=tuple((jax.ShapeDtypeStruct(r.shape,...]
    pallas_call x1, Pallas kernels: 24.6 us -> 23.8 us  [body(): pl.pallas_call(functools.partial(kernel, narrow, wide, vectors, comps, nx...]
where the time goes in v3:
time: 36.8 us; the launch traced here: 36.3 us
  Pallas kernels  25.4 us (69%)
  local copies, waits for them, and re-layouts  10.2 us (28%)
  between operations  0.67 us (2%)
    pallas_call x1, Pallas kernels, body(): pl.pallas_call(functools.partial(kernel, narrow, wide, vectors, comps, nx...  23.8 us
    unnamed x26, local copies, waits for them, and re-layouts  10.2 us
    pallas_call x1, Pallas kernels, body(): pl.pallas_call(write_out, out_shape=tuple((jax.ShapeDtypeStruct(r.shape,...  1.59 us

profile of v3, /device:TPU:0, one launch (start us, length us, event | category | flops | bytes accessed | tf_op | source)
XLA Modules:
  0.0 36.3 jit_solution(10344916836114077408)
XLA Ops:
  0.6 0.0 copy-start
  0.6 1.4 %copy-done = bf16[12,12,3,5,256]{4,2,3,1,0:T(4,128)(2,1)S(1)} copy-done((bf16[12,12,3,5,256]{4,2,3,1,0:T(4,128)(2,1)S(1)}, bf16[12,12,3,5,256]{4,2,3,1,0:T(4,128)(2,1)}, u32[]{:S(2)}) %copy-start) | copy-done | bytes 1105944
  2.0 0.0 copy-start.1
  2.0 1.0 %copy-done.1 = bf16[8,3,4,8,256]{4,3,2,1,0:T(8,128)(2,1)S(1)} copy-done((bf16[8,3,4,8,256]{4,3,2,1,0:T(8,128)(2,1)S(1)}, bf16[8,3,4,8,256]{4,3,2,1,0:T(8,128)(2,1)}, u32[]{:S(2)}) %copy-start.1) | copy-done | bytes 393240
  3.0 0.0 copy-start.2
  3.0 1.0 %copy-done.2 = s32[192,288]{1,0:T(8,128)S(1)} copy-done((s32[192,288]{1,0:T(8,128)S(1)}, s32[192,288]{1,0:T(8,128)}, u32[]{:S(2)}) %copy-start.2) | copy-done | bytes 221208
  4.0 0.0 copy-start.3
  4.0 0.9 %copy-done.3 = f32[3,4,8,256]{3,2,1,0:T(8,128)S(1)} copy-done((f32[3,4,8,256]{3,2,1,0:T(8,128)S(1)}, f32[3,4,8,256]{3,2,1,0:T(8,128)}, u32[]{:S(2)}) %copy-start.3) | copy-done | bytes 98328
  4.9 0.0 copy-start.5
  4.9 0.8 %copy-done.5 = f32[4,8,256]{2,1,0:T(8,128)S(1)} copy-done((f32[4,8,256]{2,1,0:T(8,128)S(1)}, f32[4,8,256]{2,1,0:T(8,128)}, u32[]{:S(2)}) %copy-start.5) | copy-done | bytes 32792
  5.6 0.0 copy-start.6
  5.6 0.8 %copy-done.6 = f32[4,8,256]{2,1,0:T(8,128)S(1)} copy-done((f32[4,8,256]{2,1,0:T(8,128)S(1)}, f32[4,8,256]{2,1,0:T(8,128)}, u32[]{:S(2)}) %copy-start.6) | copy-done | bytes 32792
  6.4 0.0 copy-start.8
  6.4 0.7 %copy-done.8 = f32[8,256]{1,0:T(8,128)S(1)} copy-done((f32[8,256]{1,0:T(8,128)S(1)}, f32[8,256]{1,0:T(8,128)}, u32[]{:S(2)}) %copy-start.8) | copy-done | bytes 8216
  7.1 0.0 copy-start.9
  7.1 0.7 %copy-done.9 = f32[27,3,3]{0,2,1:T(4,128)S(1)} copy-done((f32[27,3,3]{0,2,1:T(4,128)S(1)}, f32[27,3,3]{0,2,1:T(4,128)}, u32[]{:S(2)}) %copy-start.9) | copy-done | bytes 996
  7.8 0.7 %copy-done.10 = s32[1,1,2,2]{3,2,1,0:T(2,128)S(1)} copy-done((s32[1,1,2,2]{3,2,1,0:T(2,128)S(1)}, s32[1,1,2,2]{3,2,1,0:T(2,128)}, u32[]{:S(2)}) %copy-start.10) | copy-done | bytes 40
  8.4 0.7 %copy-done.12 = s32[1,1,9]{2,1,0:T(1,128)S(1)} copy-done((s32[1,1,9]{2,1,0:T(1,128)S(1)}, s32[1,1,9]{2,1,0:T(1,128)}, u32[]{:S(2)}) %copy-start.12) | copy-done | bytes 60
  9.1 23.8 %shard_map.121 = (f32[3,4,8,256]{3,2,1,0:T(8,128)S(1)}, f32[1,1,8,8,9]{4,3,2,1,0:T(8,128)S(1)}, f32[1,256]{1,0:T(1,128)S(1)}) custom-call(bf16[8,3,4,8,256]{4,3,2,1,0:T(8,128)(2,1)S(1)} %copy-done.1, f32[3,4,8,256]{3,2,1,0:T(8,128)S(1)} %copy-done.3, f32[4,8,256]{2,1,0:T(8,128)S(1)} %copy-done.5, f32[4,8,256]{2,1,0:T(8,128)S(1)} %copy-done.6, ...), custom_call_target="tpu_custom_call" | custom-call | tf_op jit(solution)/shard_map/pallas_call | solution.py:565
  32.9 0.0 copy-start.4
  32.9 0.6 %copy-done.4 = f32[3,4,8,256]{3,2,1,0:T(8,128)} copy-done((f32[3,4,8,256]{3,2,1,0:T(8,128)}, f32[3,4,8,256]{3,2,1,0:T(8,128)S(1)}, u32[]{:S(2)}) %copy-start.4) | copy-done | bytes 98328
  33.6 0.6 %copy-done.7 = f32[1,1,8,8,9]{4,3,2,1,0:T(8,128)} copy-done((f32[1,1,8,8,9]{4,3,2,1,0:T(8,128)}, f32[1,1,8,8,9]{4,3,2,1,0:T(8,128)S(1)}, u32[]{:S(2)}) %copy-start.7) | copy-done | bytes 2328
  34.2 0.5 %copy-done.11 = f32[1,256]{1,0:T(1,128)} copy-done((f32[1,256]{1,0:T(1,128)}, f32[1,256]{1,0:T(1,128)S(1)}, u32[]{:S(2)}) %copy-start.11) | copy-done | bytes 1048
  34.7 1.6 %shard_map.122 = (f32[3,4,8,256]{3,2,1,0:T(8,128)}, f32[1,1,8,8,9]{4,3,2,1,0:T(8,128)}, f32[1,256]{1,0:T(1,128)}) custom-call(f32[3,4,8,256]{3,2,1,0:T(8,128)} %copy-done.4, f32[1,1,8,8,9]{4,3,2,1,0:T(8,128)} %copy-done.7, f32[1,256]{1,0:T(1,128)} %copy-done.11), custom_call_target="tpu_custom_call" | custom-call | tf_op jit(solution)/shard_map/pallas_call | solution.py:613
  (4 shorter events, 0.0 us)
Async XLA Ops:
  0.6 1.4 %copy-start = (bf16[12,12,3,5,256]{4,2,3,1,0:T(4,128)(2,1)S(1)}, bf16[12,12,3,5,256]{4,2,3,1,0:T(4,128)(2,1)}, u32[]{:S(2)}) copy-start(bf16[12,12,3,5,256]{4,2,3,1,0:T(4,128)(2,1)} %param.15) | copy-start | bytes 3317764
  2.0 1.0 %copy-start.1 = (bf16[8,3,4,8,256]{4,3,2,1,0:T(8,128)(2,1)S(1)}, bf16[8,3,4,8,256]{4,3,2,1,0:T(8,128)(2,1)}, u32[]{:S(2)}) copy-start(bf16[8,3,4,8,256]{4,3,2,1,0:T(8,128)(2,1)} %deflation.1) | copy-start | bytes 1179652
  3.0 1.0 %copy-start.2 = (s32[192,288]{1,0:T(8,128)S(1)}, s32[192,288]{1,0:T(8,128)}, u32[]{:S(2)}) copy-start(s32[192,288]{1,0:T(8,128)} %constant.2.clone.places) | copy-start | bytes 663556
  4.0 0.9 %copy-start.3 = (f32[3,4,8,256]{3,2,1,0:T(8,128)S(1)}, f32[3,4,8,256]{3,2,1,0:T(8,128)}, u32[]{:S(2)}) copy-start(f32[3,4,8,256]{3,2,1,0:T(8,128)} %residual.1) | copy-start | bytes 294916
  4.9 0.8 %copy-start.5 = (f32[4,8,256]{2,1,0:T(8,128)S(1)}, f32[4,8,256]{2,1,0:T(8,128)}, u32[]{:S(2)}) copy-start(f32[4,8,256]{2,1,0:T(8,128)} %stiffness.1) | copy-start | bytes 98308
  5.6 0.8 %copy-start.6 = (f32[4,8,256]{2,1,0:T(8,128)S(1)}, f32[4,8,256]{2,1,0:T(8,128)}, u32[]{:S(2)}) copy-start(f32[4,8,256]{2,1,0:T(8,128)} %mass.1) | copy-start | bytes 98308
  6.4 0.7 %copy-start.8 = (f32[8,256]{1,0:T(8,128)S(1)}, f32[8,256]{1,0:T(8,128)}, u32[]{:S(2)}) copy-start(f32[8,256]{1,0:T(8,128)} %factor.1) | copy-start | bytes 24580
  7.1 0.7 %copy-start.9 = (f32[27,3,3]{0,2,1:T(4,128)S(1)}, f32[27,3,3]{0,2,1:T(4,128)}, u32[]{:S(2)}) copy-start(f32[27,3,3]{0,2,1:T(4,128)} %param.14) | copy-start | bytes 2920
  7.8 0.7 %copy-start.10 = (s32[1,1,2,2]{3,2,1,0:T(2,128)S(1)}, s32[1,1,2,2]{3,2,1,0:T(2,128)}, u32[]{:S(2)}) copy-start(s32[1,1,2,2]{3,2,1,0:T(2,128)} %margins.1) | copy-start | bytes 52
  8.4 0.7 %copy-start.12 = (s32[1,1,9]{2,1,0:T(1,128)S(1)}, s32[1,1,9]{2,1,0:T(1,128)}, u32[]{:S(2)}) copy-start(s32[1,1,9]{2,1,0:T(1,128)} %listing.1) | copy-start | bytes 112
  32.9 0.6 %copy-start.4 = (f32[3,4,8,256]{3,2,1,0:T(8,128)}, f32[3,4,8,256]{3,2,1,0:T(8,128)S(1)}, u32[]{:S(2)}) copy-start(f32[3,4,8,256]{3,2,1,0:T(8,128)S(1)} %get-tuple-element.9.refs_0_) | copy-start | bytes 294916
  33.6 0.6 %copy-start.7 = (f32[1,1,8,8,9]{4,3,2,1,0:T(8,128)}, f32[1,1,8,8,9]{4,3,2,1,0:T(8,128)S(1)}, u32[]{:S(2)}) copy-start(f32[1,1,8,8,9]{4,3,2,1,0:T(8,128)S(1)} %get-tuple-element.10.refs_1_) | copy-start | bytes 6916
  34.2 0.5 %copy-start.11 = (f32[1,256]{1,0:T(1,128)}, f32[1,256]{1,0:T(1,128)S(1)}, u32[]{:S(2)}) copy-start(f32[1,256]{1,0:T(1,128)S(1)} %get-tuple-element.11.refs_2_) | copy-start | bytes 3076

commit v4 on v3

--- a/solution.py
+++ b/solution.py
@@ -10,7 +10,6 @@
 
 F32 = jnp.float32
 BF16 = jnp.bfloat16
-HIGHEST = lax.Precision.HIGHEST
 MESH = pl.DeviceIdType.MESH
 
 
@@ -68,6 +67,16 @@
     return sum((values >= k * size).astype(jnp.int32) for k in range(1, count))
 
 
+def exact_dot(values, chosen):
+    rows = values.shape[0]
+    high = values.astype(BF16).astype(F32)
+    middle = (values - high).astype(BF16).astype(F32)
+    low = values - high - middle
+    parts = jnp.concatenate([high, middle, low], axis=0).astype(BF16)
+    product = jnp.dot(parts, chosen.astype(BF16), preferred_element_type=F32)
+    return product[:rows] + product[rows : 2 * rows] + product[2 * rows :]
+
+
 def gram(left, right):
     dims = (((1,), (1,)), ((), ()))
     high, low = split(left)
@@ -84,70 +93,83 @@
     nx,
     ny,
     depth,
-    deflation,
-    residual,
-    stiffness,
-    mass,
-    places,
-    stencil,
-    inverse_hbm,
-    factor,
-    margins,
-    listing,
-    out,
-    blocks_out,
-    solution_out,
-    inverse,
-    d32,
-    r32,
-    t32,
-    s_parts,
-    stage,
-    ext,
-    loc,
-    send_x,
-    send_y,
-    send_c,
-    recv_x,
-    recv_y,
-    recv_c,
-    factors,
-    message,
-    slots,
-    inverse_sem,
-    send_sems,
-    recv_sems,
-    wave_send,
-    wave_recv,
+    *refs,
 ):
-    n = narrow * wide
+    operands, results = refs[:10], refs[10:13]
+    held, staged = refs[13:23], refs[23:26]
+    deflation, residual, stiffness, mass, places, stencil = held[:6]
+    inverse, factor, margins, listing = held[6:]
+    out, blocks_out, solution_out = staged
+    (
+        d32,
+        r32,
+        t32,
+        s_parts,
+        stage,
+        ext,
+        loc,
+        send_x,
+        send_y,
+        send_c,
+        recv_x,
+        recv_y,
+        recv_c,
+        factors,
+        message,
+        partial,
+        slots_narrow,
+        slots_wide,
+        in_sems,
+        out_sems,
+        send_sems,
+        recv_sems,
+        wave_send,
+        wave_recv,
+    ) = refs[26:]
     order = factor.shape[1]
     row = lax.axis_index("narrow")
     column = lax.axis_index("wide")
-    me = row * wide + column
     cells = nx * ny
     own_rows = comps * cells
 
+    fetches = [
+        pltpu.make_async_copy(source, target, in_sems.at[k])
+        for k, (source, target) in enumerate(zip(operands, held))
+    ]
+    for fetch in fetches:
+        fetch.start()
+
     def turned(here, count):
-        places_of = [here + k for k in range(count)]
+        places_of = [here + k for k in range(1, count)]
         return [jnp.where(at >= count, at - count, at) for at in places_of]
 
-    target_rows = turned(row, narrow)
-
-    target_columns = turned(column, wide)
-
-    def to_others(act, step=1):
-        for k in range(step, n, step):
-            act(k // step - 1, (target_rows[k // wide], target_columns[k % wide]))
+    along_narrow = [(at, column) for at in turned(row, narrow)]
+    along_wide = [(row, at) for at in turned(column, wide)]
+    diagonals = [(x, y) for x in (-1, 1) for y in (-1, 1)]
+
+    def inside(shift_x, shift_y):
+        along_x = (row + shift_x >= 0) & (row + shift_x < narrow)
+        along_y = (column + shift_y >= 0) & (column + shift_y < wide)
+        return along_x & along_y
+
     barrier = pltpu.get_barrier_semaphore()
 
-    def greet(k, device):
+    def greet(device):
         pl.semaphore_signal(barrier, inc=1, device_id=device, device_id_type=MESH)
 
-    to_others(greet)
-
-    inverse_copy = pltpu.make_async_copy(inverse_hbm, inverse, inverse_sem)
-    inverse_copy.start()
+    greetings = narrow - 1 + wide - 1
+    for device in along_narrow + along_wide:
+        greet(device)
+    for shift_x, shift_y in diagonals:
+        greetings += jnp.where(inside(shift_x, shift_y), 1, 0)
+
+        @pl.when(inside(shift_x, shift_y))
+        def _(shift_x=shift_x, shift_y=shift_y):
+            greet((row + shift_x, column + shift_y))
+
+    for k, fetch in enumerate(fetches):
+        if k != 6:
+            fetch.wait()
 
     rounded = residual[...].astype(BF16).astype(F32).reshape(own_rows, depth)
     store(r32, rounded, pl.ds(0, own_rows))
@@ -219,35 +241,55 @@
         value = jnp.zeros(here.shape, F32)
         for e in range(comps * 9) if j is None else range(j * 9, j * 9 + 9):
             value = jnp.where(here == e, coupling[e], value)
-        s_parts[pl.ds(start, size), :] = value
-    s_high, s_low = split(s_parts[...])
-
-    pl.semaphore_wait(barrier, n - 1)
-
-    def wave(number):
-        def one(k, device):
+        s_parts[pl.ds(start, size), pl.ds(0, 3 * own_rows)] = value
+    high, low = split(s_parts[:, pl.ds(0, 3 * own_rows)])
+    s_parts[:, pl.ds(3 * own_rows, 3 * own_rows)] = high.astype(F32)
+    s_parts[:, pl.ds(6 * own_rows, 3 * own_rows)] = low.astype(F32)
+    s_all = s_parts[...].astype(BF16)
+
+    pl.semaphore_wait(barrier, greetings)
+
+    def spread_out(source, landing, sem, devices):
+        for k, device in enumerate(devices):
             pltpu.make_async_remote_copy(
-                src_ref=message.at[number],
-                dst_ref=slots.at[number, k],
-                send_sem=wave_send.at[number],
-                recv_sem=wave_recv.at[number],
+                src_ref=source,
+                dst_ref=landing(k),
+                send_sem=wave_send.at[sem],
+                recv_sem=wave_recv.at[sem],
                 device_id=device,
                 device_id_type=MESH,
             ).start()
 
-        to_others(one)
-
-    def wave_sum(number):
-        pltpu.make_async_copy(slots.at[number], slots.at[number], wave_recv.at[number]).wait()
-        return lax.fori_loop(
-            0,
-            n - 1,
-            lambda k, total: total + slots[number, k],
-            message[number],
-            unroll=n <= 32,
-        )
-
-    wave(0)
+    def await_all(ref, sems, sem):
+        pltpu.make_async_copy(ref, ref, sems.at[sem]).wait()
+
+    def summed(ref, number, start):
+        for k in range(ref.shape[1]):
+            start = start + ref[number, k]
+        return start
+
+    def wave_start(number):
+        landing = lambda k: slots_narrow.at[number, k]
+        spread_out(message.at[number], landing, 2 * number, along_narrow)
+
+    def wave_middle(number):
+        await_all(slots_narrow.at[number], wave_recv, 2 * number)
+        partial[number] = summed(slots_narrow, number, message[number])
+        landing = lambda k: slots_wide.at[number, k]
+        spread_out(partial.at[number], landing, 2 * number + 1, along_wide)
+
+    def wave_end(number):
+        await_all(slots_wide.at[number], wave_recv, 2 * number + 1)
+        return summed(slots_wide, number, partial[number])
+
+    wave_start(0)
+
+    parity = lax.rem(column, 2)
+    half_column = column // 2
+    factors[parity, half_column, row] = factor[...]
+    spread_out(factor, lambda k: factors.at[parity, half_column, row], 4, along_narrow)
+    narrow_rows = factors.at[0, 0, pl.ds(0, narrow - 1)]
+    wide_rows = factors.at[0, pl.ds(0, wide // 2 - 1)]
 
     def copies():
         found = []
@@ -263,11 +305,6 @@
 
     opposite = (1, 0, 3, 2, 7, 6, 5, 4)
 
-    def inside(shift_x, shift_y):
-        along_x = (row + shift_x >= 0) & (row + shift_x < narrow)
-        along_y = (column + shift_y >= 0) & (column + shift_y < wide)
-        return along_x & along_y
-
     def face_copy(k, source, target, shift_x, shift_y):
         return pltpu.make_async_remote_copy(
             src_ref=source,
@@ -284,27 +321,6 @@
         def _(k=k, source=source, target=target, shift_x=shift_x, shift_y=shift_y):
             face_copy(k, source, target, shift_x, shift_y).start()
 
-    parity = lax.rem(column, 2)
-    half_index = row * (wide // 2) + column // 2
-    partner = (row, column + 1 - 2 * parity)
-    factors[parity, half_index] = factor[...]
-
-    def send_factor(k, device):
-        pltpu.make_async_remote_copy(
-            src_ref=factor,
-            dst_ref=factors.at[parity, half_index],
-            send_sem=wave_send.at[2],
-            recv_sem=wave_recv.at[2],
-            device_id=device,
-            device_id_type=MESH,
-        ).start()
-
-    to_others(send_factor, 2)
-
-    def others_rows():
-        some = factors.at[0, pl.ds(0, n // 2 - 1)]
-        return some, some
-
     lane = iota((own_rows, depth), 1)
     scale = jnp.concatenate([stiffness[...].reshape(cells, depth)] * comps, axis=0)
     weight = jnp.concatenate([mass[...].reshape(cells, depth)] * comps, axis=0)
@@ -315,27 +331,26 @@
         before = jnp.where(lane == depth - 1, 0.0, pltpu.roll(w, depth - 1, axis=1))
         after = jnp.where(lane == 0, 0.0, pltpu.roll(w, 1, axis=1))
         parts = [split(shifted) for shifted in (before, w, after)]
-        high = jnp.concatenate([part[0] for part in parts], axis=0)
-        low = jnp.concatenate([part[1] for part in parts], axis=0)
-        image = (
-            jnp.dot(s_high, high, preferred_element_type=F32)
-            + jnp.dot(s_high, low, preferred_element_type=F32)
-            + jnp.dot(s_low, high, preferred_element_type=F32)
-        )
+        highs, lows = [part[0] for part in parts], [part[1] for part in parts]
+        w_all = jnp.concatenate(highs + lows + highs, axis=0)
+        image = jnp.dot(s_all, w_all, preferred_element_type=F32)
         t32[a, pl.ds(own_rows, total_rows - own_rows), :] = image[own_rows:]
         t32[a, pl.ds(0, own_rows), :] = image[:own_rows] + weight * d
         return carry
 
-    lax.fori_loop(0, vectors, adjoint, 0, unroll=2)
-
-    some, same = others_rows()
-    pltpu.make_async_copy(some, same, wave_recv.at[2]).wait()
+    lax.fori_loop(0, vectors // 2, adjoint, 0, unroll=2)
+    wave_middle(0)
+    await_all(narrow_rows, wave_recv, 4)
+    mine = factors.at[parity, half_column]
+    spread_out(mine, lambda k: mine, 5, along_wide[1::2])
+    lax.fori_loop(vectors // 2, vectors, adjoint, 0, unroll=2)
+    await_all(wide_rows, wave_recv, 5)
     hand_on = pltpu.make_async_remote_copy(
         src_ref=factors.at[parity],
         dst_ref=factors.at[parity],
-        send_sem=wave_send.at[3],
-        recv_sem=wave_recv.at[3],
-        device_id=partner,
+        send_sem=wave_send.at[6],
+        recv_sem=wave_recv.at[6],
+        device_id=(row, column + 1 - 2 * parity),
         device_id_type=MESH,
     )
     hand_on.start()
@@ -351,7 +366,7 @@
     def folded(values, lane_of):
         rows = values.shape[1]
         chosen = (lane_of(iota((rows, 1), 0)) == iota((rows, width), 1)).astype(F32)
-        return jnp.dot(values, chosen, preferred_element_type=F32, precision=HIGHEST)
+        return exact_dot(values, chosen)
 
     def within(size):
         return lambda c: c - size * quotient(c, size, vectors)
@@ -419,6 +434,11 @@
 
     blocks += folded(picked(part, corner_row, c_padded), corner_lane)
 
+    out_copies = [
+        pltpu.make_async_copy(source, target, out_sems.at[k])
+        for k, (source, target) in enumerate(zip(staged, results))
+    ]
+
     pairs = vectors * vectors
     repeated = jnp.broadcast_to(blocks[:, None, :], (vectors, vectors, width))
     right = iota((1, vectors, width), 2)
@@ -426,21 +446,22 @@
     kept = jnp.where(right == iota((1, vectors, width), 1), repeated, 0.0).reshape(pairs, width)
     neighbour = quotient(iota((width, 1), 0), vectors, 9)
     to_lane = (neighbour == iota((width, 9), 1)).astype(F32)
-    turned_blocks = jnp.dot(kept, to_lane, preferred_element_type=F32, precision=HIGHEST)
+    turned_blocks = exact_dot(kept, to_lane)
     blocks_out[0, 0] = turned_blocks.reshape(vectors, vectors, 9)
-
-    coarse_rhs = wave_sum(0)
+    out_copies[1].start()
+
+    coarse_rhs = wave_end(0)
     hand_on.wait()
 
     def solve(vector):
         def one(d, total):
-            for half in range(2):
-                f = factors[half, d]
+            for k in range(2 * narrow):
+                f = factors[k // narrow, d, k % narrow]
                 total = total + f * jnp.sum(f * vector, axis=1, keepdims=True)
             return total
 
         zeros = jnp.zeros((factor.shape[0], order), F32)
-        total = lax.fori_loop(0, n // 2, one, zeros, unroll=8)
+        total = lax.fori_loop(0, wide // 2, one, zeros, unroll=4)
         return jnp.sum(total, axis=0, keepdims=True)
 
     first = solve(coarse_rhs)
@@ -449,9 +470,9 @@
         for k in range(9)
     ]
     spread = jnp.concatenate([m.astype(F32) for m in near], axis=0)
-    matrix_rows = jnp.dot(blocks, spread, preferred_element_type=F32, precision=HIGHEST)
+    matrix_rows = exact_dot(blocks, spread)
     message[1] = placed(jnp.sum(matrix_rows * first, axis=1, keepdims=True))
-    wave(1)
+    wave_start(1)
 
     high_y = ny + 2
 
@@ -486,7 +507,8 @@
     for s in range(2):
         e = 2 * iota((half_x, depth), 0) + s
         kept_x.append((e >= margins[0, 0, 0, 0]) & (e < margins[0, 0, 0, 1]))
-    inverse_copy.wait()
+    fetches[6].wait()
+    wave_middle(1)
 
     def local_row(v, carry):
         grouped = []
@@ -510,9 +532,10 @@
 
     lax.fori_loop(0, half_y, local_row, 0)
 
-    coarse_image = wave_sum(1)
+    coarse_image = wave_end(1)
     refined = first + solve(coarse_rhs - coarse_image)
     solution_out[...] = refined
+    out_copies[2].start()
     weights = jnp.sum(jnp.where(own_place, refined, 0.0), axis=1, keepdims=True)
     for j in range(comps):
         for x in range(nx):
@@ -522,9 +545,14 @@
                 value += weights[a : a + 1, :] * load(d32, pl.ds(at, ny))
             out[j, x] = value
 
+    out_copies[0].start()
     for number in range(2):
-        pltpu.make_async_copy(slots.at[number], slots.at[number], wave_send.at[number]).wait()
-    pltpu.make_async_copy(some, same, wave_send.at[2]).wait()
+        await_all(slots_narrow.at[number], wave_send, 2 * number)
+        await_all(slots_wide.at[number], wave_send, 2 * number + 1)
+    await_all(narrow_rows, wave_send, 4)
+    await_all(wide_rows, wave_send, 5)
+    for copy in out_copies:
+        copy.wait()
 
 
 def write_out(*refs):
@@ -553,52 +581,14 @@
     neighbor_blocks,
 ):
     vectors, comps, nx, ny, depth = deflation.shape
-    n = narrow * wide
     order = inverse_factor.shape[1]
     cells = nx * ny
     places = stencil_places(comps, nx, ny)
     turned_inverse = local_inverse.transpose(0, 1, 3, 2, 4)
     x_send = vectors * comps * ny + 32
     y_send = vectors * comps * nx + 16
-    vmem = pl.BlockSpec(memory_space=pltpu.VMEM)
-    smem = pl.BlockSpec(memory_space=pltpu.SMEM)
-    results = pl.pallas_call(
-        functools.partial(kernel, narrow, wide, vectors, comps, nx, ny, depth),
-        out_shape=(
-            jax.ShapeDtypeStruct(residual.shape, F32),
-            jax.ShapeDtypeStruct((1, 1, vectors, vectors, 9), F32),
-            jax.ShapeDtypeStruct((1, order), F32),
-        ),
-        in_specs=[vmem] * 5 + [smem, pl.BlockSpec(memory_space=pltpu.HBM), vmem, smem, smem],
-        out_specs=(vmem, vmem, vmem),
-        scratch_shapes=[
-            pltpu.VMEM(turned_inverse.shape, BF16),
-            pltpu.VMEM((depth // 128, vectors * comps * cells, 128), F32),
-            pltpu.VMEM((depth // 128, comps * cells, 128), F32),
-            pltpu.VMEM((vectors, places.shape[0], depth), F32),
-            pltpu.VMEM(places.shape, F32),
-            pltpu.VMEM((32, depth), F32),
-            pltpu.VMEM((depth // 128, comps * (ny + 2) * 8, 128), F32),
-            pltpu.VMEM((depth // 128, comps * (ny + 2) * 8, 128), F32),
-            pltpu.VMEM((2, x_send, depth), BF16),
-            pltpu.VMEM((2, y_send, depth), BF16),
-            pltpu.VMEM((4, 32, depth), BF16),
-            pltpu.VMEM((2, x_send, depth), BF16),
-            pltpu.VMEM((2, y_send, depth), BF16),
-            pltpu.VMEM((4, 32, depth), BF16),
-            pltpu.VMEM((2, n // 2) + inverse_factor.shape, F32),
-            pltpu.VMEM((2, 1, order), F32),
-            pltpu.VMEM((2, n - 1, 1, order), F32),
-            pltpu.SemaphoreType.DMA,
-            pltpu.SemaphoreType.DMA((8,)),
-            pltpu.SemaphoreType.DMA((8,)),
-            pltpu.SemaphoreType.DMA((4,)),
-            pltpu.SemaphoreType.DMA((4,)),
-        ],
-        compiler_params=pltpu.CompilerParams(
-            collective_id=0, has_side_effects=True, vmem_limit_bytes=40 * 1024 * 1024
-        ),
-    )(
+    anywhere = pl.BlockSpec(memory_space=pl.ANY)
+    operands = (
         deflation,
         residual,
         stiffness,
@@ -610,12 +600,56 @@
         margin_range,
         neighbor_blocks,
     )
+    spaces = [pltpu.VMEM] * 5 + [pltpu.SMEM] + [pltpu.VMEM] * 2 + [pltpu.SMEM] * 2
+    shapes = (
+        jax.ShapeDtypeStruct(residual.shape, F32),
+        jax.ShapeDtypeStruct((1, 1, vectors, vectors, 9), F32),
+        jax.ShapeDtypeStruct((1, order), F32),
+    )
+    results = pl.pallas_call(
+        functools.partial(kernel, narrow, wide, vectors, comps, nx, ny, depth),
+        out_shape=shapes,
+        in_specs=[anywhere] * len(operands),
+        out_specs=(anywhere,) * len(shapes),
+        scratch_shapes=[space(o.shape, o.dtype) for space, o in zip(spaces, operands)]
+        + [pltpu.VMEM(shape.shape, shape.dtype) for shape in shapes]
+        + [
+            pltpu.VMEM((depth // 128, vectors * comps * cells, 128), F32),
+            pltpu.VMEM((depth // 128, comps * cells, 128), F32),
+            pltpu.VMEM((vectors, places.shape[0], depth), F32),
+            pltpu.VMEM((places.shape[0], 9 * comps * cells), F32),
+            pltpu.VMEM((32, depth), F32),
+            pltpu.VMEM((depth // 128, comps * (ny + 2) * 8, 128), F32),
+            pltpu.VMEM((depth // 128, comps * (ny + 2) * 8, 128), F32),
+            pltpu.VMEM((2, x_send, depth), BF16),
+            pltpu.VMEM((2, y_send, depth), BF16),
+            pltpu.VMEM((4, 32, depth), BF16),
+            pltpu.VMEM((2, x_send, depth), BF16),
+            pltpu.VMEM((2, y_send, depth), BF16),
+            pltpu.VMEM((4, 32, depth), BF16),
+            pltpu.VMEM((2, wide // 2, narrow) + inverse_factor.shape, F32),
+            pltpu.VMEM((2, 1, order), F32),
+            pltpu.VMEM((2, 1, order), F32),
+            pltpu.VMEM((2, narrow - 1, 1, order), F32),
+            pltpu.VMEM((2, wide - 1, 1, order), F32),
+            pltpu.SemaphoreType.DMA((len(operands),)),
+            pltpu.SemaphoreType.DMA((len(shapes),)),
+            pltpu.SemaphoreType.DMA((8,)),
+            pltpu.SemaphoreType.DMA((8,)),
+            pltpu.SemaphoreType.DMA((7,)),
+            pltpu.SemaphoreType.DMA((7,)),
+        ],
+        compiler_params=pltpu.CompilerParams(
+            collective_id=0, has_side_effects=True, vmem_limit_bytes=60 * 1024 * 1024
+        ),
+    )(*operands)
     result, blocks, refined = pl.pallas_call(
         write_out,
         out_shape=tuple(jax.ShapeDtypeStruct(r.shape, r.dtype) for r in results),
-        in_specs=[vmem] * 3,
-        out_specs=tuple(pl.BlockSpec(memory_space=pltpu.HBM) for _ in results),
+        in_specs=[anywhere] * 3,
+        out_specs=(anywhere,) * 3,
         scratch_shapes=[pltpu.SemaphoreType.DMA((3,))],
+        compiler_params=pltpu.CompilerParams(vmem_limit_bytes=60 * 1024 * 1024),
     )(*results)
     return result, blocks.transpose(0, 1, 4, 2, 3), refined.reshape(order)
 

time: 36.8 us -> 29.2 us (0.79)
  local copies, waits for them, and re-layouts: 10.2 us -> 0 us
  Pallas kernels: 25.4 us -> 28.4 us
    unnamed x26 -> x0, local copies, waits for them, and re-layouts: 10.2 us -> none
    pallas_call x1, Pallas kernels: 1.59 us -> 5.13 us  [body(): pl.pallas_call(write_out, out_shape=tuple((jax.ShapeDtypeStruct(r.shape,...]
    pallas_call x1, Pallas kernels: 23.8 us -> 23.2 us  [body(): pl.pallas_call(functools.partial(kernel, narrow, wide, vectors, comps, nx...]
where the time goes in v4:
time: 29.2 us; the launch traced here: 29 us
  Pallas kernels  28.4 us (97%)
  between operations  0.64 us (2%)
    pallas_call x1, Pallas kernels, body(): pl.pallas_call(functools.partial(kernel, narrow, wide, vectors, comps, nx...  23.2 us
    pallas_call x1, Pallas kernels, body(): pl.pallas_call(write_out, out_shape=tuple((jax.ShapeDtypeStruct(r.shape,...  5.13 us

profile of v4, /device:TPU:0, one launch (start us, length us, event | category | flops | bytes accessed | tf_op | source)
XLA Modules:
  0.0 29.0 jit_solution(11746059000659963536)
XLA Ops:
  0.6 23.2 %shard_map.121 = (f32[3,4,8,256]{3,2,1,0:T(8,128)}, f32[1,1,8,8,9]{4,3,2,1,0:T(8,128)}, f32[1,256]{1,0:T(1,128)}) custom-call(bf16[8,3,4,8,256]{4,3,2,1,0:T(8,128)(2,1)} %refs_0_.1, f32[3,4,8,256]{3,2,1,0:T(8,128)} %refs_1_.1, f32[4,8,256]{2,1,0:T(8,128)} %refs_2_.1, f32[4,8,256]{2,1,0:T(8,128)} %refs_3_.1, s32[192,288]{1,0:T(8,128)} %constant.2.clone.refs_4_, ...), custom_call_target="tpu_custom_call" | custom-call | tf_op jit(solution)/shard_map/pallas_call | solution.py:609
  23.9 5.1 %shard_map.122 = (f32[3,4,8,256]{3,2,1,0:T(8,128)}, f32[1,1,8,8,9]{4,3,2,1,0:T(8,128)}, f32[1,256]{1,0:T(1,128)}) custom-call(f32[3,4,8,256]{3,2,1,0:T(8,128)} %get-tuple-element.9.refs_0_, f32[1,1,8,8,9]{4,3,2,1,0:T(8,128)} %get-tuple-element.10.refs_1_, f32[1,256]{1,0:T(1,128)} %get-tuple-element.11.refs_2_), custom_call_target="tpu_custom_call" | custom-call | tf_op jit(solution)/shard_map/pallas_call | solution.py:646

commit v5 on v4

--- a/solution.py
+++ b/solution.py
@@ -220,6 +220,80 @@
             stage[pl.ds(vectors * comps, comps), :] = load(r32, pl.ds(at, comps, stride=cells))
             send_c[side_x * 2 + side_y] = stage[...].astype(BF16)
 
+    pl.semaphore_wait(barrier, greetings)
+
+    def spread_out(source, landing, sem, devices):
+        for k, device in enumerate(devices):
+            pltpu.make_async_remote_copy(
+                src_ref=source,
+                dst_ref=landing(k),
+                send_sem=wave_send.at[sem],
+                recv_sem=wave_recv.at[sem],
+                device_id=device,
+                device_id_type=MESH,
+            ).start()
+
+    def await_all(ref, sems, sem):
+        pltpu.make_async_copy(ref, ref, sems.at[sem]).wait()
+
+    def summed(ref, number, start):
+        for k in range(ref.shape[1]):
+            start = start + ref[number, k]
+        return start
+
+    def wave_start(number):
+        landing = lambda k: slots_narrow.at[number, k]
+        spread_out(message.at[number], landing, 2 * number, along_narrow)
+
+    def wave_middle(number):
+        await_all(slots_narrow.at[number], wave_recv, 2 * number)
+        partial[number] = summed(slots_narrow, number, message[number])
+        landing = lambda k: slots_wide.at[number, k]
+        spread_out(partial.at[number], landing, 2 * number + 1, along_wide)
+
+    def wave_end(number):
+        await_all(slots_wide.at[number], wave_recv, 2 * number + 1)
+        return summed(slots_wide, number, partial[number])
+
+    wave_start(0)
+
+    parity = lax.rem(column, 2)
+    half_column = column // 2
+    factors[parity, half_column, row] = factor[...]
+    spread_out(factor, lambda k: factors.at[parity, half_column, row], 4, along_narrow)
+    narrow_rows = factors.at[0, 0, pl.ds(0, narrow - 1)]
+    wide_rows = factors.at[0, pl.ds(0, wide // 2 - 1)]
+
+    def copies():
+        found = []
+        for side, shift in enumerate((-1, 1)):
+            found.append((send_x.at[side], recv_x.at[1 - side], recv_x.at[side], shift, 0))
+        for side, shift in enumerate((-1, 1)):
+            found.append((send_y.at[side], recv_y.at[1 - side], recv_y.at[side], 0, shift))
+        for side_x, shift_x in enumerate((-1, 1)):
+            for side_y, shift_y in enumerate((-1, 1)):
+                at = side_x * 2 + side_y
+                found.append((send_c.at[at], recv_c.at[3 - at], recv_c.at[at], shift_x, shift_y))
+        return found
+
+    opposite = (1, 0, 3, 2, 7, 6, 5, 4)
+
+    def face_copy(k, source, target, shift_x, shift_y):
+        return pltpu.make_async_remote_copy(
+            src_ref=source,
+            dst_ref=target,
+            send_sem=send_sems.at[k],
+            recv_sem=recv_sems.at[opposite[k]],
+            device_id=(row + shift_x, column + shift_y),
+            device_id_type=MESH,
+        )
+
+    for k, (source, target, _, shift_x, shift_y) in enumerate(copies()):
+
+        @pl.when(inside(shift_x, shift_y))
+        def _(k=k, source=source, target=target, shift_x=shift_x, shift_y=shift_y):
+            face_copy(k, source, target, shift_x, shift_y).start()
+
     total_rows = places.shape[0]
     fixed = own_rows + 2 * x_rows
     group = quotient(iota((1, 3 * own_rows), 1), cells, 3 * comps)
@@ -247,80 +321,6 @@
     s_parts[:, pl.ds(6 * own_rows, 3 * own_rows)] = low.astype(F32)
     s_all = s_parts[...].astype(BF16)
 
-    pl.semaphore_wait(barrier, greetings)
-
-    def spread_out(source, landing, sem, devices):
-        for k, device in enumerate(devices):
-            pltpu.make_async_remote_copy(
-                src_ref=source,
-                dst_ref=landing(k),
-                send_sem=wave_send.at[sem],
-                recv_sem=wave_recv.at[sem],
-                device_id=device,
-                device_id_type=MESH,
-            ).start()
-
-    def await_all(ref, sems, sem):
-        pltpu.make_async_copy(ref, ref, sems.at[sem]).wait()
-
-    def summed(ref, number, start):
-        for k in range(ref.shape[1]):
-            start = start + ref[number, k]
-        return start
-
-    def wave_start(number):
-        landing = lambda k: slots_narrow.at[number, k]
-        spread_out(message.at[number], landing, 2 * number, along_narrow)
-
-    def wave_middle(number):
-        await_all(slots_narrow.at[number], wave_recv, 2 * number)
-        partial[number] = summed(slots_narrow, number, message[number])
-        landing = lambda k: slots_wide.at[number, k]
-        spread_out(partial.at[number], landing, 2 * number + 1, along_wide)
-
-    def wave_end(number):
-        await_all(slots_wide.at[number], wave_recv, 2 * number + 1)
-        return summed(slots_wide, number, partial[number])
-
-    wave_start(0)
-
-    parity = lax.rem(column, 2)
-    half_column = column // 2
-    factors[parity, half_column, row] = factor[...]
-    spread_out(factor, lambda k: factors.at[parity, half_column, row], 4, along_narrow)
-    narrow_rows = factors.at[0, 0, pl.ds(0, narrow - 1)]
-    wide_rows = factors.at[0, pl.ds(0, wide // 2 - 1)]
-
-    def copies():
-        found = []
-        for side, shift in enumerate((-1, 1)):
-            found.append((send_x.at[side], recv_x.at[1 - side], recv_x.at[side], shift, 0))
-        for side, shift in enumerate((-1, 1)):
-            found.append((send_y.at[side], recv_y.at[1 - side], recv_y.at[side], 0, shift))
-        for side_x, shift_x in enumerate((-1, 1)):
-            for side_y, shift_y in enumerate((-1, 1)):
-                at = side_x * 2 + side_y
-                found.append((send_c.at[at], recv_c.at[3 - at], recv_c.at[at], shift_x, shift_y))
-        return found
-
-    opposite = (1, 0, 3, 2, 7, 6, 5, 4)
-
-    def face_copy(k, source, target, shift_x, shift_y):
-        return pltpu.make_async_remote_copy(
-            src_ref=source,
-            dst_ref=target,
-            send_sem=send_sems.at[k],
-            recv_sem=recv_sems.at[opposite[k]],
-            device_id=(row + shift_x, column + shift_y),
-            device_id_type=MESH,
-        )
-
-    for k, (source, target, _, shift_x, shift_y) in enumerate(copies()):
-
-        @pl.when(inside(shift_x, shift_y))
-        def _(k=k, source=source, target=target, shift_x=shift_x, shift_y=shift_y):
-            face_copy(k, source, target, shift_x, shift_y).start()
-
     lane = iota((own_rows, depth), 1)
     scale = jnp.concatenate([stiffness[...].reshape(cells, depth)] * comps, axis=0)
     weight = jnp.concatenate([mass[...].reshape(cells, depth)] * comps, axis=0)
@@ -382,7 +382,6 @@
         ).astype(BF16)
         part = gram(left, right)
         total = part if total is None else total + part
-    blocks = folded(picked(total, within(cells), cells), lane_in(4, cells))
 
     for k, (source, target, landing, shift_x, shift_y) in enumerate(copies()):
 
@@ -401,36 +400,99 @@
         def _(landing=landing):
             landing[...] = jnp.zeros(landing.shape, BF16)
 
+    y_padded = pad_to(y_rows, 8)
+    c_padded = pad_to(4 * comps, 8)
+
+    def corner_parts(c):
+        corner = quotient(c, 32, 4)
+        at = c - 32 * corner
+        vector = quotient(at, comps, vectors)
+        return at < vectors * comps, corner, vector, at - comps * vector
+
+    def corner_row(c):
+        real, corner, _, j = corner_parts(c)
+        return jnp.where(real, corner * comps + j, -1)
+
+    def corner_lane(c):
+        real, corner, vector, _ = corner_parts(c)
+        block = corner * 2 + jnp.where(corner >= 2, 2, 0)
+        return jnp.where(real, block * vectors + vector, -1)
+
+    coarse_rhs = wave_end(0)
+    hand_on.wait()
+
+    def solve(vector):
+        def one(d, total):
+            for k in range(2 * narrow):
+                f = factors[k // narrow, d, k % narrow]
+                total = total + f * jnp.sum(f * vector, axis=1, keepdims=True)
+            return total
+
+        zeros = jnp.zeros((factor.shape[0], order), F32)
+        total = lax.fori_loop(0, wide // 2, one, zeros, unroll=4)
+        return jnp.sum(total, axis=0, keepdims=True)
+
+    first = solve(coarse_rhs)
+    near = [
+        iota((vectors, order), 1) == listing[0, 0, k] * vectors + iota((vectors, order), 0)
+        for k in range(9)
+    ]
+    parts_of = [jnp.sum(jnp.where(m, first, 0.0), axis=1, keepdims=True) for m in near]
+
+    def weights_on(lanes, block):
+        chosen = iota((vectors, lanes.shape[1]), 0) == lanes
+        return jnp.sum(jnp.where(chosen, parts_of[block], 0.0), axis=0, keepdims=True)
+
+    def mixed(values, weights, row_of, count):
+        lanes = iota((1, values.shape[0]), 1)
+        matrix = jnp.where(iota((count, values.shape[0]), 0) == row_of(lanes), weights, 0.0)
+        high = matrix.astype(BF16).astype(F32)
+        both = jnp.concatenate([high, matrix - high], axis=0).astype(BF16)
+        product = jnp.dot(both, values, preferred_element_type=F32)
+        return product[:count] + product[count:]
+
+    field = parts_of[4][0:1, :] * load(d32, rows_of(0))
+    for b in range(1, vectors):
+        field += parts_of[4][b : b + 1, :] * load(d32, rows_of(b))
+    fields = [field]
+    for side, block in enumerate((1, 7)):
+        lanes = quotient(iota((1, vectors * x_rows), 1), x_rows, vectors)
+        values = recv_x[side, pl.ds(0, vectors * x_rows), :]
+        fields.append(mixed(values, weights_on(lanes, block), within(x_rows), x_rows))
+    for side, block in enumerate((3, 5)):
+        lanes = quotient(iota((1, vectors * y_rows), 1), y_rows, vectors)
+        values = recv_y[side, pl.ds(0, vectors * y_rows), :]
+        fields.append(mixed(values, weights_on(lanes, block), within(y_rows), y_padded))
+    real, corner, vector, _ = corner_parts(iota((1, 4 * 32), 1))
+    weights = jnp.zeros((1, 4 * 32), F32)
+    for k, block in enumerate((0, 2, 6, 8)):
+        weights += weights_on(jnp.where(real & (corner == k), vector, -1), block)
+    fields.append(mixed(recv_c[...].reshape(4 * 32, depth), weights, corner_row, c_padded))
+    field = jnp.concatenate(fields, axis=0)
+
+    def imaged(a, carry):
+        stage[pl.ds(a, 1), :] = jnp.sum(t32[a] * field, axis=0, keepdims=True)
+        return carry
+
+    lax.fori_loop(0, vectors, imaged, 0, unroll=2)
+    message[1] = placed(jnp.sum(stage[pl.ds(0, vectors), :], axis=1, keepdims=True))
+    wave_start(1)
+
+    blocks = folded(picked(total, within(cells), cells), lane_in(4, cells))
     for side in range(2):
         block = 1 if side == 0 else 7
         left = t32[:, pl.ds(own_rows + side * x_rows, x_rows), :].reshape(vectors * x_rows, depth)
         part = gram(left, recv_x[side, pl.ds(0, vectors * x_rows), :])
         blocks += folded(picked(part, within(x_rows), x_rows), lane_in(block, x_rows))
-    y_padded = pad_to(y_rows, 8)
+    wave_middle(1)
     for side in range(2):
         block = 3 if side == 0 else 5
         left = t32[:, pl.ds(fixed + side * y_padded, y_padded), :]
         left = left.reshape(vectors * y_padded, depth)
         part = gram(left, recv_y[side, pl.ds(0, vectors * y_rows), :])
         blocks += folded(picked(part, within(y_rows), y_padded), lane_in(block, y_rows))
-    c_padded = pad_to(4 * comps, 8)
     left = t32[:, pl.ds(fixed + 2 * y_padded, c_padded), :].reshape(vectors * c_padded, depth)
     part = gram(left, recv_c[...].reshape(4 * 32, depth))
-
-    def corner_parts(c):
-        corner = quotient(c, 32, 4)
-        at = c - 32 * corner
-        vector = quotient(at, comps, vectors)
-        return at < vectors * comps, corner, vector, at - comps * vector
-
-    def corner_row(c):
-        real, corner, _, j = corner_parts(c)
-        return jnp.where(real, corner * comps + j, -1)
-
-    def corner_lane(c):
-        real, corner, vector, _ = corner_parts(c)
-        block = corner * 2 + jnp.where(corner >= 2, 2, 0)
-        return jnp.where(real, block * vectors + vector, -1)
 
     blocks += folded(picked(part, corner_row, c_padded), corner_lane)
 
@@ -449,30 +511,6 @@
     turned_blocks = exact_dot(kept, to_lane)
     blocks_out[0, 0] = turned_blocks.reshape(vectors, vectors, 9)
     out_copies[1].start()
-
-    coarse_rhs = wave_end(0)
-    hand_on.wait()
-
-    def solve(vector):
-        def one(d, total):
-            for k in range(2 * narrow):
-                f = factors[k // narrow, d, k % narrow]
-                total = total + f * jnp.sum(f * vector, axis=1, keepdims=True)
-            return total
-
-        zeros = jnp.zeros((factor.shape[0], order), F32)
-        total = lax.fori_loop(0, wide // 2, one, zeros, unroll=4)
-        return jnp.sum(total, axis=0, keepdims=True)
-
-    first = solve(coarse_rhs)
-    near = [
-        iota((vectors, order), 1) == listing[0, 0, k] * vectors + iota((vectors, order), 0)
-        for k in range(9)
-    ]
-    spread = jnp.concatenate([m.astype(F32) for m in near], axis=0)
-    matrix_rows = exact_dot(blocks, spread)
-    message[1] = placed(jnp.sum(matrix_rows * first, axis=1, keepdims=True))
-    wave_start(1)
 
     high_y = ny + 2
 
@@ -508,7 +546,6 @@
         e = 2 * iota((half_x, depth), 0) + s
         kept_x.append((e >= margins[0, 0, 0, 0]) & (e < margins[0, 0, 0, 1]))
     fetches[6].wait()
-    wave_middle(1)
 
     def local_row(v, carry):
         grouped = []
@@ -646,7 +683,7 @@
     result, blocks, refined = pl.pallas_call(
         write_out,
         out_shape=tuple(jax.ShapeDtypeStruct(r.shape, r.dtype) for r in results),
-        in_specs=[anywhere] * 3,
+        in_specs=[pl.BlockSpec(memory_space=pltpu.VMEM)] * 3,
         out_specs=(anywhere,) * 3,
         scratch_shapes=[pltpu.SemaphoreType.DMA((3,))],
         compiler_params=pltpu.CompilerParams(vmem_limit_bytes=60 * 1024 * 1024),

time: 29.2 us -> 25.2 us (0.86)
  Pallas kernels: 28.4 us -> 24.3 us
    pallas_call x1, Pallas kernels: 5.13 us -> 1.59 us  [body(): pl.pallas_call(write_out, out_shape=tuple((jax.ShapeDtypeStruct(r.shape,...]
    pallas_call x1, Pallas kernels: 23.2 us -> 22.7 us  [body(): pl.pallas_call(functools.partial(kernel, narrow, wide, vectors, comps, nx...]
where the time goes in v5:
time: 25.2 us; the launch traced here: 25 us
  Pallas kernels  24.3 us (96%)
  between operations  0.64 us (3%)
    pallas_call x1, Pallas kernels, body(): pl.pallas_call(functools.partial(kernel, narrow, wide, vectors, comps, nx...  22.7 us
    pallas_call x1, Pallas kernels, body(): pl.pallas_call(write_out, out_shape=tuple((jax.ShapeDtypeStruct(r.shape,...  1.59 us

profile of v5, /device:TPU:0, one launch (start us, length us, event | category | flops | bytes accessed | tf_op | source)
XLA Modules:
  0.0 25.0 jit_solution(14445594808123971760)
XLA Ops:
  0.6 22.7 %shard_map.121 = (f32[3,4,8,256]{3,2,1,0:T(8,128)}, f32[1,1,8,8,9]{4,3,2,1,0:T(8,128)}, f32[1,256]{1,0:T(1,128)}) custom-call(bf16[8,3,4,8,256]{4,3,2,1,0:T(8,128)(2,1)} %refs_0_.1, f32[3,4,8,256]{3,2,1,0:T(8,128)} %refs_1_.1, f32[4,8,256]{2,1,0:T(8,128)} %refs_2_.1, f32[4,8,256]{2,1,0:T(8,128)} %refs_3_.1, s32[192,288]{1,0:T(8,128)} %constant.2.clone.refs_4_, ...), custom_call_target="tpu_custom_call" | custom-call | tf_op jit(solution)/shard_map/pallas_call | solution.py:646
  23.4 1.6 %shard_map.122 = (f32[3,4,8,256]{3,2,1,0:T(8,128)}, f32[1,1,8,8,9]{4,3,2,1,0:T(8,128)}, f32[1,256]{1,0:T(1,128)}) custom-call(f32[3,4,8,256]{3,2,1,0:T(8,128)} %get-tuple-element.9.refs_0_, f32[1,1,8,8,9]{4,3,2,1,0:T(8,128)} %get-tuple-element.10.refs_1_, f32[1,256]{1,0:T(1,128)} %get-tuple-element.11.refs_2_), custom_call_target="tpu_custom_call" | custom-call | tf_op jit(solution)/shard_map/pallas_call | solution.py:683

commit v6 on v5

--- a/solution.py
+++ b/solution.py
@@ -95,11 +95,10 @@
     depth,
     *refs,
 ):
-    operands, results = refs[:10], refs[10:13]
-    held, staged = refs[13:23], refs[23:26]
+    operands, held = refs[:10], refs[13:23]
     deflation, residual, stiffness, mass, places, stencil = held[:6]
     inverse, factor, margins, listing = held[6:]
-    out, blocks_out, solution_out = staged
+    out, blocks_out, solution_out = refs[10:13]
     (
         d32,
         r32,
@@ -120,12 +119,11 @@
         slots_narrow,
         slots_wide,
         in_sems,
-        out_sems,
         send_sems,
         recv_sems,
         wave_send,
         wave_recv,
-    ) = refs[26:]
+    ) = refs[23:]
     order = factor.shape[1]
     row = lax.axis_index("narrow")
     column = lax.axis_index("wide")
@@ -306,14 +304,23 @@
                 for i in range(comps):
                     line = jnp.where(lanes_of[oz * comps + i], stencil[i, j, d * 3 + oz], line)
             coupling.append(line)
-    chunks = [(j * cells, cells, j) for j in range(comps)]
+    all_j = range(comps)
+    chunks = [(j * cells, cells, range(j * 9, j * 9 + 9)) for j in all_j]
     for side in range(2):
-        chunks += [(own_rows + side * x_rows + j * ny, ny, j) for j in range(comps)]
-    chunks.append((fixed, total_rows - fixed, None))
-    for start, size, j in chunks:
+        at = own_rows + side * x_rows
+        for j in all_j:
+            dx = j * 9 + 6 * side
+            chunks.append((at + j * ny, ny, range(dx, dx + 3)))
+    y_size = pad_to(y_rows, 8)
+    for side in range(2):
+        entries = [j * 9 + 3 * dx + 2 * side for j in all_j for dx in range(3)]
+        chunks.append((fixed + side * y_size, y_size, entries))
+    corner_entries = [j * 9 + d for j in all_j for d in (0, 2, 6, 8)]
+    chunks.append((fixed + 2 * y_size, total_rows - fixed - 2 * y_size, corner_entries))
+    for start, size, entries in chunks:
         here = places[pl.ds(start, size), :]
         value = jnp.zeros(here.shape, F32)
-        for e in range(comps * 9) if j is None else range(j * 9, j * 9 + 9):
+        for e in entries:
             value = jnp.where(here == e, coupling[e], value)
         s_parts[pl.ds(start, size), pl.ds(0, 3 * own_rows)] = value
     high, low = split(s_parts[:, pl.ds(0, 3 * own_rows)])
@@ -338,12 +345,12 @@
         t32[a, pl.ds(0, own_rows), :] = image[:own_rows] + weight * d
         return carry
 
-    lax.fori_loop(0, vectors // 2, adjoint, 0, unroll=2)
+    lax.fori_loop(0, vectors // 2, adjoint, 0, unroll=4)
     wave_middle(0)
     await_all(narrow_rows, wave_recv, 4)
     mine = factors.at[parity, half_column]
     spread_out(mine, lambda k: mine, 5, along_wide[1::2])
-    lax.fori_loop(vectors // 2, vectors, adjoint, 0, unroll=2)
+    lax.fori_loop(vectors // 2, vectors, adjoint, 0, unroll=4)
     await_all(wide_rows, wave_recv, 5)
     hand_on = pltpu.make_async_remote_copy(
         src_ref=factors.at[parity],
@@ -496,11 +503,6 @@
 
     blocks += folded(picked(part, corner_row, c_padded), corner_lane)
 
-    out_copies = [
-        pltpu.make_async_copy(source, target, out_sems.at[k])
-        for k, (source, target) in enumerate(zip(staged, results))
-    ]
-
     pairs = vectors * vectors
     repeated = jnp.broadcast_to(blocks[:, None, :], (vectors, vectors, width))
     right = iota((1, vectors, width), 2)
@@ -510,7 +512,6 @@
     to_lane = (neighbour == iota((width, 9), 1)).astype(F32)
     turned_blocks = exact_dot(kept, to_lane)
     blocks_out[0, 0] = turned_blocks.reshape(vectors, vectors, 9)
-    out_copies[1].start()
 
     high_y = ny + 2
 
@@ -572,7 +573,6 @@
     coarse_image = wave_end(1)
     refined = first + solve(coarse_rhs - coarse_image)
     solution_out[...] = refined
-    out_copies[2].start()
     weights = jnp.sum(jnp.where(own_place, refined, 0.0), axis=1, keepdims=True)
     for j in range(comps):
         for x in range(nx):
@@ -582,14 +582,11 @@
                 value += weights[a : a + 1, :] * load(d32, pl.ds(at, ny))
             out[j, x] = value
 
-    out_copies[0].start()
     for number in range(2):
         await_all(slots_narrow.at[number], wave_send, 2 * number)
         await_all(slots_wide.at[number], wave_send, 2 * number + 1)
     await_all(narrow_rows, wave_send, 4)
     await_all(wide_rows, wave_send, 5)
-    for copy in out_copies:
-        copy.wait()
 
 
 def write_out(*refs):
@@ -645,11 +642,10 @@
     )
     results = pl.pallas_call(
         functools.partial(kernel, narrow, wide, vectors, comps, nx, ny, depth),
-        out_shape=shapes,
+        out_shape=tuple(pltpu.VMEM(shape.shape, shape.dtype) for shape in shapes),
         in_specs=[anywhere] * len(operands),
-        out_specs=(anywhere,) * len(shapes),
+        out_specs=(pl.BlockSpec(memory_space=pltpu.VMEM),) * len(shapes),
         scratch_shapes=[space(o.shape, o.dtype) for space, o in zip(spaces, operands)]
-        + [pltpu.VMEM(shape.shape, shape.dtype) for shape in shapes]
         + [
             pltpu.VMEM((depth // 128, vectors * comps * cells, 128), F32),
             pltpu.VMEM((depth // 128, comps * cells, 128), F32),
@@ -670,7 +666,6 @@
             pltpu.VMEM((2, narrow - 1, 1, order), F32),
             pltpu.VMEM((2, wide - 1, 1, order), F32),
             pltpu.SemaphoreType.DMA((len(operands),)),
-            pltpu.SemaphoreType.DMA((len(shapes),)),
             pltpu.SemaphoreType.DMA((8,)),
             pltpu.SemaphoreType.DMA((8,)),
             pltpu.SemaphoreType.DMA((7,)),
@@ -686,7 +681,7 @@
         in_specs=[pl.BlockSpec(memory_space=pltpu.VMEM)] * 3,
         out_specs=(anywhere,) * 3,
         scratch_shapes=[pltpu.SemaphoreType.DMA((3,))],
-        compiler_params=pltpu.CompilerParams(vmem_limit_bytes=60 * 1024 * 1024),
+        compiler_params=pltpu.CompilerParams(vmem_limit_bytes=2 * 1024 * 1024),
     )(*results)
     return result, blocks.transpose(0, 1, 4, 2, 3), refined.reshape(order)
 

time: 25.2 us -> 23.6 us (0.937)
  Pallas kernels: 24.3 us -> 22.8 us
    pallas_call x1, Pallas kernels: 1.59 us -> 0.68 us  [body(): pl.pallas_call(write_out, out_shape=tuple((jax.ShapeDtypeStruct(r.shape,...]
    pallas_call x1, Pallas kernels: 22.7 us -> 22.1 us  [body(): pl.pallas_call(functools.partial(kernel, narrow, wide, vectors, comps, nx...]
where the time goes in v6:
time: 23.6 us; the launch traced here: 23.4 us
  Pallas kernels  22.8 us (97%)
  between operations  0.64 us (3%)
    pallas_call x1, Pallas kernels, body(): pl.pallas_call(functools.partial(kernel, narrow, wide, vectors, comps, nx...  22.1 us
    pallas_call x1, Pallas kernels, body(): pl.pallas_call(write_out, out_shape=tuple((jax.ShapeDtypeStruct(r.shape,...  0.68 us

profile of v6, /device:TPU:0, one launch (start us, length us, event | category | flops | bytes accessed | tf_op | source)
XLA Modules:
  0.0 23.4 jit_solution(6224785281598057236)
XLA Ops:
  0.6 22.1 %shard_map.121 = (f32[3,4,8,256]{3,2,1,0:T(8,128)S(1)}, f32[1,1,8,8,9]{4,3,2,1,0:T(8,128)S(1)}, f32[1,256]{1,0:T(1,128)S(1)}) custom-call(bf16[8,3,4,8,256]{4,3,2,1,0:T(8,128)(2,1)} %refs_0_.1, f32[3,4,8,256]{3,2,1,0:T(8,128)} %refs_1_.1, f32[4,8,256]{2,1,0:T(8,128)} %refs_2_.1, f32[4,8,256]{2,1,0:T(8,128)} %refs_3_.1, s32[192,288]{1,0:T(8,128)} %constant.2.clone.refs_4_, ...), custom_call_target="tpu_custom_call" | custom-call | tf_op jit(solution)/shard_map/pallas_call | solution.py:643
  22.7 0.7 %shard_map.122 = (f32[3,4,8,256]{3,2,1,0:T(8,128)}, f32[1,1,8,8,9]{4,3,2,1,0:T(8,128)}, f32[1,256]{1,0:T(1,128)}) custom-call(f32[3,4,8,256]{3,2,1,0:T(8,128)S(1)} %get-tuple-element.9.refs_0_, f32[1,1,8,8,9]{4,3,2,1,0:T(8,128)S(1)} %get-tuple-element.10.refs_1_, f32[1,256]{1,0:T(1,128)S(1)} %get-tuple-element.11.refs_2_), custom_call_target="tpu_custom_call" | custom-call | tf_op jit(solution)/shard_map/pallas_call | solution.py:678

commit v7 on v6

--- a/solution.py
+++ b/solution.py
@@ -79,10 +79,10 @@
 
 def gram(left, right):
     dims = (((1,), (1,)), ((), ()))
-    high, low = split(left)
-    return lax.dot_general(high, right, dims, preferred_element_type=F32) + lax.dot_general(
-        low, right, dims, preferred_element_type=F32
-    )
+    rows = left.shape[0]
+    both = jnp.concatenate(split(left), axis=0)
+    product = lax.dot_general(both, right, dims, preferred_element_type=F32)
+    return product[:rows] + product[rows:]
 
 
 def kernel(
@@ -381,14 +381,14 @@
     def lane_in(block, size):
         return lambda c: block * vectors + quotient(c, size, vectors)
 
-    total = None
+    lefts = []
+    rights = []
     for j in range(comps):
-        left = t32[:, pl.ds(j * cells, cells), :].reshape(vectors * cells, depth)
-        right = jnp.concatenate(
-            [load(d32, pl.ds((b * comps + j) * cells, cells)) for b in range(vectors)], axis=0
-        ).astype(BF16)
-        part = gram(left, right)
-        total = part if total is None else total + part
+        left = t32[:, pl.ds(j * cells, cells), :]
+        lefts.append(left.reshape(vectors * cells, depth))
+        pieces = [load(d32, pl.ds((b * comps + j) * cells, cells)) for b in range(vectors)]
+        rights.append(jnp.concatenate(pieces, axis=0).astype(BF16))
+    total = gram(jnp.concatenate(lefts, axis=1), jnp.concatenate(rights, axis=1))
 
     for k, (source, target, landing, shift_x, shift_y) in enumerate(copies()):
 

time: 23.6 us -> 23.6 us (level)
  no operation moved by 1% of the time
where the time goes in v7:
time: 23.6 us; the launch traced here: 23.4 us
  Pallas kernels  22.8 us (97%)
  between operations  0.64 us (3%)
    pallas_call x1, Pallas kernels, body(): pl.pallas_call(functools.partial(kernel, narrow, wide, vectors, comps, nx...  22.1 us
    pallas_call x1, Pallas kernels, body(): pl.pallas_call(write_out, out_shape=tuple((jax.ShapeDtypeStruct(r.shape,...  0.68 us

profile of v7, /device:TPU:0, one launch (start us, length us, event | category | flops | bytes accessed | tf_op | source)
XLA Modules:
  0.0 23.4 jit_solution(2720982486424778024)
XLA Ops:
  0.6 22.1 %shard_map.121 = (f32[3,4,8,256]{3,2,1,0:T(8,128)S(1)}, f32[1,1,8,8,9]{4,3,2,1,0:T(8,128)S(1)}, f32[1,256]{1,0:T(1,128)S(1)}) custom-call(bf16[8,3,4,8,256]{4,3,2,1,0:T(8,128)(2,1)} %refs_0_.1, f32[3,4,8,256]{3,2,1,0:T(8,128)} %refs_1_.1, f32[4,8,256]{2,1,0:T(8,128)} %refs_2_.1, f32[4,8,256]{2,1,0:T(8,128)} %refs_3_.1, s32[192,288]{1,0:T(8,128)} %constant.2.clone.refs_4_, ...), custom_call_target="tpu_custom_call" | custom-call | tf_op jit(solution)/shard_map/pallas_call | solution.py:643
  22.7 0.7 %shard_map.122 = (f32[3,4,8,256]{3,2,1,0:T(8,128)}, f32[1,1,8,8,9]{4,3,2,1,0:T(8,128)}, f32[1,256]{1,0:T(1,128)}) custom-call(f32[3,4,8,256]{3,2,1,0:T(8,128)S(1)} %get-tuple-element.9.refs_0_, f32[1,1,8,8,9]{4,3,2,1,0:T(8,128)S(1)} %get-tuple-element.10.refs_1_, f32[1,256]{1,0:T(1,128)S(1)} %get-tuple-element.11.refs_2_), custom_call_target="tpu_custom_call" | custom-call | tf_op jit(solution)/shard_map/pallas_call | solution.py:678

commit v8 on v7

--- a/solution.py
+++ b/solution.py
@@ -169,6 +169,48 @@
         if k != 6:
             fetch.wait()
 
+    pl.semaphore_wait(barrier, greetings)
+
+    def spread_out(source, landing, sem, devices):
+        for k, device in enumerate(devices):
+            pltpu.make_async_remote_copy(
+                src_ref=source,
+                dst_ref=landing(k),
+                send_sem=wave_send.at[sem],
+                recv_sem=wave_recv.at[sem],
+                device_id=device,
+                device_id_type=MESH,
+            ).start()
+
+    def await_all(ref, sems, sem):
+        pltpu.make_async_copy(ref, ref, sems.at[sem]).wait()
+
+    def summed(ref, number, start):
+        for k in range(ref.shape[1]):
+            start = start + ref[number, k]
+        return start
+
+    def wave_start(number):
+        landing = lambda k: slots_narrow.at[number, k]
+        spread_out(message.at[number], landing, 2 * number, along_narrow)
+
+    def wave_middle(number):
+        await_all(slots_narrow.at[number], wave_recv, 2 * number)
+        partial[number] = summed(slots_narrow, number, message[number])
+        landing = lambda k: slots_wide.at[number, k]
+        spread_out(partial.at[number], landing, 2 * number + 1, along_wide)
+
+    def wave_end(number):
+        await_all(slots_wide.at[number], wave_recv, 2 * number + 1)
+        return summed(slots_wide, number, partial[number])
+
+    parity = lax.rem(column, 2)
+    half_column = column // 2
+    factors[parity, half_column, row] = factor[...]
+    spread_out(factor, lambda k: factors.at[parity, half_column, row], 4, along_narrow)
+    narrow_rows = factors.at[0, 0, pl.ds(0, narrow - 1)]
+    wide_rows = factors.at[0, pl.ds(0, wide // 2 - 1)]
+
     rounded = residual[...].astype(BF16).astype(F32).reshape(own_rows, depth)
     store(r32, rounded, pl.ds(0, own_rows))
 
@@ -218,49 +260,7 @@
             stage[pl.ds(vectors * comps, comps), :] = load(r32, pl.ds(at, comps, stride=cells))
             send_c[side_x * 2 + side_y] = stage[...].astype(BF16)
 
-    pl.semaphore_wait(barrier, greetings)
-
-    def spread_out(source, landing, sem, devices):
-        for k, device in enumerate(devices):
-            pltpu.make_async_remote_copy(
-                src_ref=source,
-                dst_ref=landing(k),
-                send_sem=wave_send.at[sem],
-                recv_sem=wave_recv.at[sem],
-                device_id=device,
-                device_id_type=MESH,
-            ).start()
-
-    def await_all(ref, sems, sem):
-        pltpu.make_async_copy(ref, ref, sems.at[sem]).wait()
-
-    def summed(ref, number, start):
-        for k in range(ref.shape[1]):
-            start = start + ref[number, k]
-        return start
-
-    def wave_start(number):
-        landing = lambda k: slots_narrow.at[number, k]
-        spread_out(message.at[number], landing, 2 * number, along_narrow)
-
-    def wave_middle(number):
-        await_all(slots_narrow.at[number], wave_recv, 2 * number)
-        partial[number] = summed(slots_narrow, number, message[number])
-        landing = lambda k: slots_wide.at[number, k]
-        spread_out(partial.at[number], landing, 2 * number + 1, along_wide)
-
-    def wave_end(number):
-        await_all(slots_wide.at[number], wave_recv, 2 * number + 1)
-        return summed(slots_wide, number, partial[number])
-
     wave_start(0)
-
-    parity = lax.rem(column, 2)
-    half_column = column // 2
-    factors[parity, half_column, row] = factor[...]
-    spread_out(factor, lambda k: factors.at[parity, half_column, row], 4, along_narrow)
-    narrow_rows = factors.at[0, 0, pl.ds(0, narrow - 1)]
-    wide_rows = factors.at[0, pl.ds(0, wide // 2 - 1)]
 
     def copies():
         found = []
@@ -345,12 +345,13 @@
         t32[a, pl.ds(0, own_rows), :] = image[:own_rows] + weight * d
         return carry
 
-    lax.fori_loop(0, vectors // 2, adjoint, 0, unroll=4)
+    cuts = (0, vectors // 4, vectors * 5 // 8, vectors)
+    lax.fori_loop(cuts[0], cuts[1], adjoint, 0, unroll=True)
     wave_middle(0)
     await_all(narrow_rows, wave_recv, 4)
     mine = factors.at[parity, half_column]
     spread_out(mine, lambda k: mine, 5, along_wide[1::2])
-    lax.fori_loop(vectors // 2, vectors, adjoint, 0, unroll=4)
+    lax.fori_loop(cuts[1], cuts[2], adjoint, 0, unroll=True)
     await_all(wide_rows, wave_recv, 5)
     hand_on = pltpu.make_async_remote_copy(
         src_ref=factors.at[parity],
@@ -361,6 +362,7 @@
         device_id_type=MESH,
     )
     hand_on.start()
+    lax.fori_loop(cuts[2], cuts[3], adjoint, 0, unroll=True)
 
     width = 9 * vectors
 

time: 23.6 us -> 23.9 us (1.013)
  Pallas kernels: 22.8 us -> 23.1 us
    pallas_call x1, Pallas kernels: 22.1 us -> 22.4 us  [body(): pl.pallas_call(functools.partial(kernel, narrow, wide, vectors, comps, nx...]
where the time goes in v8:
time: 23.9 us; the launch traced here: 23.7 us
  Pallas kernels  23.1 us (97%)
  between operations  0.64 us (3%)
    pallas_call x1, Pallas kernels, body(): pl.pallas_call(functools.partial(kernel, narrow, wide, vectors, comps, nx...  22.4 us
    pallas_call x1, Pallas kernels, body(): pl.pallas_call(write_out, out_shape=tuple((jax.ShapeDtypeStruct(r.shape,...  0.68 us

profile of v8, /device:TPU:0, one launch (start us, length us, event | category | flops | bytes accessed | tf_op | source)
XLA Modules:
  0.0 23.7 jit_solution(4359634368158231358)
XLA Ops:
  0.6 22.4 %shard_map.121 = (f32[3,4,8,256]{3,2,1,0:T(8,128)S(1)}, f32[1,1,8,8,9]{4,3,2,1,0:T(8,128)S(1)}, f32[1,256]{1,0:T(1,128)S(1)}) custom-call(bf16[8,3,4,8,256]{4,3,2,1,0:T(8,128)(2,1)} %refs_0_.1, f32[3,4,8,256]{3,2,1,0:T(8,128)} %refs_1_.1, f32[4,8,256]{2,1,0:T(8,128)} %refs_2_.1, f32[4,8,256]{2,1,0:T(8,128)} %refs_3_.1, s32[192,288]{1,0:T(8,128)} %constant.2.clone.refs_4_, ...), custom_call_target="tpu_custom_call" | custom-call | tf_op jit(solution)/shard_map/pallas_call | solution.py:645
  23.0 0.7 %shard_map.122 = (f32[3,4,8,256]{3,2,1,0:T(8,128)}, f32[1,1,8,8,9]{4,3,2,1,0:T(8,128)}, f32[1,256]{1,0:T(1,128)}) custom-call(f32[3,4,8,256]{3,2,1,0:T(8,128)S(1)} %get-tuple-element.9.refs_0_, f32[1,1,8,8,9]{4,3,2,1,0:T(8,128)S(1)} %get-tuple-element.10.refs_1_, f32[1,256]{1,0:T(1,128)S(1)} %get-tuple-element.11.refs_2_), custom_call_target="tpu_custom_call" | custom-call | tf_op jit(solution)/shard_map/pallas_call | solution.py:680
